TPU v7x, 256 devices: a whole 4x4x8 slice. The times are simulated.
256 devices in a mesh: row: 16 (over z_hi, y), col: 16 (over z_lo, x, core).
Axes of the slice: x: 4, y: 4, z: 8 (z_hi: 4, z_lo: 2; z = z_hi * 2 + z_lo), core: 2. Of those that a mesh axis runs over, the one named last changes fastest.
Arguments:
- out_grad: bfloat16 [65536, 128], P(('row', 'col')), may hold values from -6 to 6
- preact: bfloat16 [65536, 128], P(('row', 'col')), may hold values from -6 to 6
- aggregated: bfloat16 [65536, 128], P(('row', 'col')), may hold values from -6 to 6
- weight: bfloat16 [128, 128], replicated, may hold values from -0.5 to 0.5
- tiles: bfloat16 [16, 16, 256, 128, 128], P('row', 'col'), may hold values from -0.09375 to 0.09375
- tile_coords: int32 [16, 16, 2, 256], P('row', 'col'), may hold values from 0 to 31, as said below
- tile_count: int32 [16, 16], P('row', 'col'), may hold values from 32 to 256, as said below
Outputs:
- input_grad: bfloat16 [65536, 128], P(('row', 'col'))
- weight_grad: float32 [128, 128], replicated
Inputs may be any that keep to these rules, and one draw needn't show every extreme that they name: `tile_coords`: on each device the first tile_count slots hold distinct tiles, in non-decreasing row block; row blocks are below 32 and column blocks below 32; entries of later slots are not used. `tile_count`: some device uses all 256 slots.
All inputs are finite; a program needn't handle non-finite values.
Results may differ from a plain program's by a relative error of at most 0.0049.
Values may be sent and summed in bfloat16 or wider, within the bound.
No kernel may reach another device: no remote copies, remote signals or barrier semaphores. Data moves between devices by JAX's collectives and lax.ppermute only.
A program may use at most 64 MiB of HBM per device.

v0:
```python
import functools

import jax
import jax.numpy as jnp
from jax import lax
from jax.experimental import pallas as pl
from jax.experimental.pallas import tpu as pltpu
from jax.sharding import Mesh, PartitionSpec as P

bf16 = jnp.bfloat16
f32 = jnp.float32
i32 = jnp.int32
T = 128
ROWS = ("zh", "y")
COLS = ("zl", "x", "core")
BLOCKS = 32
SLOTS = 256
STRIDE = 320
PLACES = 1024
PART = 16
UNROLL = 32
NOWHERE = 31
LIMIT = 16 * 1024 * 1024


def spec(space=pltpu.VMEM):
    return pl.BlockSpec(memory_space=space)


def split_parts(value):
    high = value.astype(bf16)
    low = (value - high.astype(f32)).astype(bf16)
    return high, low


def ring_sum(own, received):
    return (own + received[1]) + (received[0] + received[2])


def local_kernel(inputs, message):
    n = (inputs.shape[0] - T) // 3
    og, pre, agg = (inputs[pl.ds(i * n, n), :] for i in range(3))
    weight = inputs[3 * n :, :]
    grad_pre = jnp.where(pre > 0, og, jnp.zeros_like(og))
    message[0:T, :] = lax.dot_general(
        weight, grad_pre, (((1,), (1,)), ((), ())), preferred_element_type=f32
    ).astype(bf16)
    partial = lax.dot_general(
        agg, grad_pre, (((0,), (0,)), ((), ())), preferred_element_type=f32
    )
    high, low = split_parts(partial)
    message[T : 2 * T, 0:T] = high
    message[T : 2 * T, T : 2 * T] = low


def chip_kernel(pos, own, other, message):
    core = pos[4]
    message[pl.ds(pl.multiple_of(core * T, T), T), :] = own[0:T, :]
    message[pl.ds(pl.multiple_of((1 - core) * T, T), T), :] = other[0:T, :]
    sums = [m[T : 2 * T, 0:T].astype(f32) + m[T : 2 * T, T : 2 * T].astype(f32) for m in (own, other)]
    total = (sums[0] + sums[1]).astype(bf16)
    message[2 * T : 2 * T + 64, 0:T] = total[0:64, :]
    message[2 * T : 2 * T + 64, T : 2 * T] = total[64:T, :]


def order_kernel(pos, count_ref, coords_hbm, tiles_hbm, out, tiles, coords, sems):
    fetches = [
        pltpu.make_async_copy(tiles_hbm.at[part], tiles.at[part], sems.at[1 + i])
        for i, part in enumerate(pl.ds(g * PART, PART) for g in range(SLOTS // PART))
    ]
    fetch_coords = pltpu.make_async_copy(coords_hbm, coords, sems.at[0])
    fetch_coords.start()
    count, y = count_ref[0], pos[1]
    for g, fetch in enumerate(fetches):
        pl.when(g * PART < count)(fetch.start)
    fetch_coords.wait()
    zh, turn = pos[0], 1 - 2 * pos[4]

    def place(k, ends):
        row, col = coords[0, k], coords[1, k]
        offset = ((((col >> 1) & 3) - y) * turn) & 3
        z_place = (((col >> 3) - zh) * turn + 2) & 3
        local = z_place * 2 + (col & 1) + jnp.where(offset == 3, 8, 0)
        stage = jnp.where(offset == 2, 0, jnp.where(offset == 0, 2, 1))
        end = jnp.where(offset == 2, ends[0], jnp.where(offset == 0, ends[2], ends[1]))
        out[0, end] = k + (row << 8) + (local << 16)
        return tuple(e + (stage == i).astype(i32) for i, e in enumerate(ends))

    starts = tuple(jnp.int32(STRIDE * i) for i in range(3))
    step = 8
    whole = count // step

    def several(i, ends):
        for u in range(step):
            ends = place(i * step + u, ends)
        return ends

    ends = lax.fori_loop(0, whole, several, starts)
    ends = lax.fori_loop(whole * step, count, place, ends)
    for i in range(3):
        for u in range(UNROLL):
            out[0, ends[i] + u] = NOWHERE << 16
        out[0, STRIDE * 3 + i] = (ends[i] - STRIDE * i + UNROLL - 1) // UNROLL
    for g, fetch in enumerate(fetches):
        pl.when(g * PART < count)(fetch.wait)


def multiply(stage, order, grads, tiles, acc):
    acc[...] = jnp.zeros_like(acc)
    spare = acc.shape[0] - 1

    @pl.loop(0, order[0, STRIDE * 3 + stage])
    def _(group):
        for u in range(UNROLL):
            code = order[0, STRIDE * stage + group * UNROLL + u]
            at = jnp.minimum(code >> 16, spare)
            acc[at] += jnp.dot(
                grads[(code >> 8) & 31], tiles[code & 255], preferred_element_type=f32
            )


def first_kernel(pos, order, *refs):
    mine, got, swapped = refs[0], refs[1:5], refs[5:9]
    tiles, grads, weight_part, send, acc, parts = refs[9:]
    zl, x, core = pos[2], pos[3], pos[4]

    arrived = [(got[k], core, k) for k in range(4)]
    arrived += [(swapped[k], 1 - core, k) for k in range(4)]
    arrived += [(mine, 0, 0)]
    for message, side, k in arrived:
        chip = ((zl + side) & 1) * 4 + ((x - k * (1 - 2 * side)) & 3)
        for c in range(2):
            for h in range(2):
                grads[chip * 4 + 2 * c + h] = message[c * T : (c + 1) * T, h * T : (h + 1) * T]
        parts[chip] = message[2 * T : 2 * T + 64, :]
    total = parts[0].astype(f32)
    for chip in range(1, 8):
        total += parts[chip].astype(f32)
    rounded = total.astype(bf16)
    weight_part[0:64, :] = rounded[:, 0:T]
    weight_part[64:T, :] = rounded[:, T : 2 * T]
    multiply(0, order, grads, tiles, acc)
    for i in range(8):
        send[i * T : (i + 1) * T, :] = acc[i].astype(bf16)
    send[8 * T : 9 * T, :] = weight_part[...]


def second_kernel(order, grads, weight_part, tiles, early_1, late_1, early_3, late_3, acc):
    multiply(1, order, grads, tiles, acc)
    for first, early, late in ((0, early_1, late_1), (8, early_3, late_3)):
        for i in range(4):
            early[i * T : (i + 1) * T, :] = acc[first + i].astype(bf16)
            late[i * T : (i + 1) * T, :] = acc[first + 4 + i].astype(bf16)
        early[4 * T : 5 * T, :] = weight_part[...]


def third_kernel(order, grads, tiles, after, early, late, acc):
    del after
    multiply(2, order, grads, tiles, acc)
    for i in range(4):
        early[i * T : (i + 1) * T, :] = acc[i]
        late[i * T : (i + 1) * T, :] = acc[4 + i]


def early_kernel(own, weight_part, r1, r2, r3, send_2, send_3, weight_y):
    parts = [r1[4 * T : 5 * T, :], r2[8 * T : 9 * T, :], r3[4 * T : 5 * T, :]]
    rounded = ring_sum(weight_part[...].astype(f32), [p.astype(f32) for p in parts]).astype(bf16)
    weight_y[...] = rounded
    for i, out in enumerate((send_2, send_3)):
        rows = pl.ds(i * 2 * T, 2 * T)
        total = own[rows, :]
        for r in (r1, r2, r3):
            total += r[rows, :].astype(f32)
        out[0 : 2 * T, :] = total.astype(bf16)
        out[2 * T : 3 * T, :] = rounded


def late_kernel(own, weight_y, r1, r2, r3, keep, send_1):
    for i, out in enumerate((keep, send_1)):
        rows = pl.ds(i * 2 * T, 2 * T)
        total = own[rows, :] + r2[(i + 2) * 2 * T : (i + 3) * 2 * T, :].astype(f32)
        for r in (r1, r3):
            total += r[rows, :].astype(f32)
        out[0 : 2 * T, :] = total.astype(out.dtype)
    send_1[2 * T : 3 * T, :] = weight_y[...]


def z_kernel(scale, keep, weight_y, r1, r2, r3, out, weight_out):
    parts = [r[2 * T : 3 * T, :].astype(f32) for r in (r1, r2, r3)]
    weight_out[...] = ring_sum(weight_y[...].astype(f32), parts) * scale
    for h in range(2):
        rows = pl.ds(h * T, T)
        total = keep[rows, :]
        for r in (r1, r2, r3):
            total += r[rows, :].astype(f32)
        out[rows, :] = total.T.astype(bf16)


def call(kernel, out_shape, in_specs, scratch=(), cost=None, out_specs=None):
    return pl.pallas_call(
        kernel,
        out_shape=out_shape,
        in_specs=in_specs,
        out_specs=out_specs or jax.tree.map(lambda _: spec(), out_shape),
        scratch_shapes=list(scratch),
        compiler_params=pltpu.CompilerParams(vmem_limit_bytes=LIMIT),
        cost_estimate=cost,
    )


def struct(*shape, dtype=bf16):
    return jax.ShapeDtypeStruct(shape, dtype)


def around(axis, value, d):
    pairs = [(i * 2, ((i + d) % 4) * 2) for i in range(4)]
    pairs += [(i * 2 + 1, ((i - d) % 4) * 2 + 1) for i in range(4)]
    return lax.ppermute(value, (axis, "core"), pairs)


def chip_perm(k):
    pairs = []
    for z in range(2):
        for x in range(4):
            at = (z * 4 + x) * 2
            if k:
                pairs.append((at, (z * 4 + (x + k) % 4) * 2))
            pairs.append((at + 1, ((1 - z) * 4 + (x - k) % 4) * 2 + 1))
    return pairs


def body(out_grad, preact, aggregated, weight, tiles, tile_coords, tile_count):
    smem, vmem, hbm = spec(pltpu.SMEM), spec(), spec(pltpu.HBM)
    nodes = out_grad.shape[0]
    pos = jnp.stack([lax.axis_index(a) for a in ROWS + COLS]).astype(i32)
    inputs = jnp.concatenate([out_grad, preact, aggregated, weight], 0)
    swap = [(0, 1), (1, 0)]
    local = call(local_kernel, struct(2 * T, nodes), [vmem])(inputs)
    mine = call(chip_kernel, struct(2 * T + 64, nodes), [smem, vmem, vmem])(
        pos, local, lax.ppermute(local, "core", swap)
    )
    order, held = call(
        order_kernel,
        [pltpu.SMEM((1, PLACES), i32), pltpu.VMEM((SLOTS, T, T), bf16)],
        [smem, smem, hbm, hbm],
        [pltpu.SMEM((2, SLOTS), i32), pltpu.SemaphoreType.DMA((1 + SLOTS // PART,))],
        pl.CostEstimate(flops=0, bytes_accessed=2 * SLOTS * T * T * 2, transcendentals=0),
        (smem, vmem),
    )(
        pos,
        tile_count.reshape(1),
        pltpu.with_memory_space_constraint(tile_coords.reshape(2, SLOTS), pltpu.HBM),
        pltpu.with_memory_space_constraint(tiles.reshape(SLOTS, T, T), pltpu.HBM),
    )
    got = [lax.ppermute(mine, COLS, chip_perm(k)) for k in range(4)]
    swapped = []
    for k in range(4):
        ready = got[k]
        if k == 3:
            ready, _ = lax.optimization_barrier((ready, order))
        swapped.append(lax.ppermute(ready, "core", swap))
    cost = lambda share: pl.CostEstimate(
        flops=share * SLOTS * 2 * T**3, bytes_accessed=share * SLOTS * T * T * 2, transcendentals=0
    )
    early, late, onward = struct(5 * T, T), struct(4 * T, T), struct(3 * T, T)
    grads, weight_part, send_2 = call(
        first_kernel,
        [struct(BLOCKS, T, T), struct(T, T), struct(9 * T, T)],
        [smem] * 2 + [vmem] * 10,
        [pltpu.VMEM((9, T, T), f32), pltpu.VMEM((8, 64, 2 * T), bf16)],
        cost(1),
    )(pos, order, mine, *got, *swapped, held)
    early_1, late_1, early_3, late_3 = call(
        second_kernel,
        [early, late] * 2,
        [smem] + [vmem] * 3,
        [pltpu.VMEM((17, T, T), f32)],
        cost(1),
    )(order, grads, weight_part, held)
    got_2 = around("y", send_2, 2)
    own_early, own_late = call(
        third_kernel,
        [struct(4 * T, T, dtype=f32)] * 2,
        [smem] + [vmem] * 2 + [spec(pl.ANY)],
        [pltpu.VMEM((9, T, T), f32)],
        cost(1),
    )(order, grads, held, early_1)
    got_early = [around("y", early_1, 1), got_2, around("y", early_3, 3)]
    got_late = [around("y", late_1, 1), got_2, around("y", late_3, 3)]
    send_2, send_3, weight_y = call(
        early_kernel, [onward, onward, struct(T, T)], [vmem] * 5, cost=cost(10)
    )(own_early, weight_part, *got_early)
    z_2, z_3 = around("zh", send_2, 2), around("zh", send_3, 3)
    keep, send_1 = call(late_kernel, [struct(2 * T, T, dtype=f32), onward], [vmem] * 5)(
        own_late, weight_y, *got_late
    )
    z_1 = around("zh", send_1, 1)
    devices = 1
    for a in ROWS + COLS:
        devices *= lax.axis_size(a)
    scale = 1.0 / (nodes * devices) ** 0.5
    input_grad, weight_grad = call(
        functools.partial(z_kernel, scale),
        [struct(nodes, T), struct(T, T, dtype=f32)],
        [vmem] * 5,
    )(keep, weight_y, z_1, z_2, z_3)
    return input_grad, weight_grad


def solution(mesh):
    fine = Mesh(mesh.devices.reshape(4, 4, 2, 4, 2), ROWS + COLS)
    every = ROWS + COLS
    return jax.shard_map(
        body,
        mesh=fine,
        in_specs=(
            P(every, None),
            P(every, None),
            P(every, None),
            P(),
            P(ROWS, COLS, None, None, None),
            P(ROWS, COLS, None, None),
            P(ROWS, COLS),
        ),
        out_specs=(P(every, None), P()),
        check_vma=False,
    )
```

profile of v0, /device:TPU:1, one launch (start us, length us, event | category | flops | bytes accessed | tf_op | source)
XLA Modules:
  0.0 54.0 jit_solution(16745888239667774976)
XLA Ops:
  0.6 0.9 %pad_maximum_fusion.inputs = bf16[896,128]{1,0:T(8,128)(2,1)S(1)} fusion(bf16[128,128]{1,0:T(8,128)(2,1)} %param.10, bf16[256,128]{1,0:T(8,128)(2,1)} %param.9, bf16[256,128]{1,0:T(8,128)(2,1)} %param.8, bf16[256,128]{1,0:T(8,128)(2,1)} %param.7), kind=kLoop, calls=%fused_computation | loop fusion | flops 917504 | bytes 458752 | tf_op jit(solution)/shard_map/concatenate | solution.py:236
  1.6 0.2 shard_map.87.own
  1.8 3.3 %collective-permute-start = (bf16[256,256]{1,0:T(8,128)(2,1)S(1)}, bf16[256,256]{1,0:T(8,128)(2,1)S(1)}, u32[]{:S(2)}, u32[]{:S(2)}) collective-permute-start(bf16[256,256]{1,0:T(8,128)(2,1)S(1)} %shard_map.87.own), channel_id=1, source_target_pairs={{0,1},{1,0},{2,3},{3,2},{4,5},{5,4},{6,7},{7,6},{8,9},{9,8},{10,11... | collective-permute-start | bytes 393224 | tf_op jit(solution)/shard_map/ppermute | solution.py:240
  5.1 0.1 stack.23.pos
  5.2 0.9 %collective-permute-done.other = bf16[256,256]{1,0:T(8,128)(2,1)S(1)} collective-permute-done((bf16[256,256]{1,0:T(8,128)(2,1)S(1)}, bf16[256,256]{1,0:T(8,128)(2,1)S(1)}, u32[]{:S(2)}, u32[]{:S(2)}) %collective-permute-start) | collective-permute-done | bytes 131104 | tf_op jit(solution)/shard_map/ppermute | solution.py:240
  6.1 0.6 %shard_map.88.refs_0_ = bf16[320,256]{1,0:T(8,128)(2,1)S(1)} custom-call(s32[5]{0:T(128)S(1)} %stack.23.pos, bf16[256,256]{1,0:T(8,128)(2,1)S(1)} %shard_map.87.own, bf16[256,256]{1,0:T(8,128)(2,1)S(1)} %collective-permute-done.other), custom_call_target="tpu_custom_call" | custom-call | tf_op jit(solution)/shard_map/pallas_call | solution.py:239
  6.7 0.9 %collective-permute-start.4 = (bf16[320,256]{1,0:T(8,128)(2,1)S(1)}, bf16[320,256]{1,0:T(8,128)(2,1)S(1)}, u32[]{:S(2)}, u32[]{:S(2)}) collective-permute-start(bf16[320,256]{1,0:T(8,128)(2,1)S(1)} %shard_map.88.refs_0_), channel_id=1, source_target_pairs={{0,6},{1,11},{2,0},{3,13},{4,2},{5,15},{6,4},{7,9},{8,14},{9,3},{1... | collective-permute-start | bytes 491528 | tf_op jit(solution)/shard_map/ppermute | solution.py:255
  7.6 2.0 %collective-permute-start.3 = (bf16[320,256]{1,0:T(8,128)(2,1)S(1)}, bf16[320,256]{1,0:T(8,128)(2,1)S(1)}, u32[]{:S(2)}, u32[]{:S(2)}) collective-permute-start(bf16[320,256]{1,0:T(8,128)(2,1)S(1)} %shard_map.88.refs_0_), channel_id=1, source_target_pairs={{0,4},{1,13},{2,6},{3,15},{4,0},{5,9},{6,2},{7,11},{8,12},{9,5},{1... | collective-permute-start | bytes 491528 | tf_op jit(solution)/shard_map/ppermute | solution.py:255
  9.6 2.5 %collective-permute-start.2 = (bf16[320,256]{1,0:T(8,128)(2,1)S(1)}, bf16[320,256]{1,0:T(8,128)(2,1)S(1)}, u32[]{:S(2)}, u32[]{:S(2)}) collective-permute-start(bf16[320,256]{1,0:T(8,128)(2,1)S(1)} %shard_map.88.refs_0_), channel_id=1, source_target_pairs={{0,2},{1,15},{2,4},{3,9},{4,6},{5,11},{6,0},{7,13},{8,10},{9,7},{1... | collective-permute-start | bytes 491528 | tf_op jit(solution)/shard_map/ppermute | solution.py:255
  12.1 1.9 %collective-permute-start.1 = (bf16[320,256]{1,0:T(8,128)(2,1)S(1)}, bf16[320,256]{1,0:T(8,128)(2,1)S(1)}, u32[]{:S(2)}, u32[]{:S(2)}) collective-permute-start(bf16[320,256]{1,0:T(8,128)(2,1)S(1)} %shard_map.88.refs_0_), channel_id=1, source_target_pairs={{1,9},{3,11},{5,13},{7,15},{9,1},{11,3},{13,5},{15,7},{17,25},{19,... | collective-permute-start | bytes 491528 | tf_op jit(solution)/shard_map/ppermute | solution.py:255
  14.7 2.0 %shard_map.86 = (s32[1,1024]{1,0:T(1,128)S(4)}, bf16[256,128,128]{2,1,0:T(8,128)(2,1)S(1)}) custom-call(s32[5]{0:T(128)S(1)} %stack.23.pos, s32[1]{0:T(128)} %bitcast.8.count_ref, s32[2,256]{1,0:T(2,128)} %bitcast.10, bf16[256,128,128]{2,1,0:T(8,128)(2,1)} %bitcast.9), custom_call_target="tpu_custom_call" | custom-call | bytes 16777216 | tf_op jit(solution)/shard_map/pallas_call | solution.py:242
  16.6 0.7 %collective-permute-start.7 = (bf16[320,256]{1,0:T(8,128)(2,1)S(1)}, bf16[320,256]{1,0:T(8,128)(2,1)S(1)}, u32[]{:S(2)}, u32[]{:S(2)}) collective-permute-start(bf16[320,256]{1,0:T(8,128)(2,1)S(1)} %collective-permute-done.3.refs_3_), channel_id=1, source_target_pairs={{0,1},{1,0},{2,3},{3,2},{4,5},{5,4},{6,7},{7,6},{8,9},{9,8},{10,11... | collective-permute-start | bytes 491528 | tf_op jit(solution)/shard_map/ppermute | solution.py:261
  17.3 1.6 %collective-permute-start.6 = (bf16[320,256]{1,0:T(8,128)(2,1)S(1)}, bf16[320,256]{1,0:T(8,128)(2,1)S(1)}, u32[]{:S(2)}, u32[]{:S(2)}) collective-permute-start(bf16[320,256]{1,0:T(8,128)(2,1)S(1)} %collective-permute-done.2.refs_2_), channel_id=1, source_target_pairs={{0,1},{1,0},{2,3},{3,2},{4,5},{5,4},{6,7},{7,6},{8,9},{9,8},{10,11... | collective-permute-start | bytes 491528 | tf_op jit(solution)/shard_map/ppermute | solution.py:261
  19.0 0.5 collective-permute-start.8
  19.5 0.5 collective-permute-done.6.refs_6_
  20.0 0.4 collective-permute-done.5.refs_5_
  20.4 0.2 collective-permute-done.8.refs_8_
  20.6 1.3 %shard_map.89 = (bf16[32,128,128]{2,1,0:T(8,128)(2,1)S(1)}, bf16[128,128]{1,0:T(8,128)(2,1)S(1)}, bf16[1152,128]{1,0:T(8,128)(2,1)S(1)}) custom-call(s32[5]{0:T(128)S(1)} %stack.23.pos, s32[1,1024]{1,0:T(1,128)S(4)} %get-tuple-element.19.order, bf16[320,256]{1,0:T(8,128)(2,1)S(1)} %shard_map.88.refs_0_, bf16[320,256]{1,0:T(8,128)(2,1)S(1)} %collective-permute-done.1.refs_1_, ...), custom_call_target="tpu_custom_call" | custom-call | flops 1073741824 | bytes 8388608 | tf_op jit(solution)/shard_map/pallas_call | solution.py:266
  22.0 2.4 %collective-permute-start.10 = (bf16[1152,128]{1,0:T(8,128)(2,1)S(1)}, bf16[1152,128]{1,0:T(8,128)(2,1)S(1)}, u32[]{:S(2)}, u32[]{:S(2)}) collective-permute-start(bf16[1152,128]{1,0:T(8,128)(2,1)S(1)} %get-tuple-element.27), channel_id=1, source_target_pairs={{0,32},{16,48},{32,0},{48,16},{1,33},{17,49},{33,1},{49,17},{2,34}... | collective-permute-start | bytes 884744 | tf_op jit(solution)/shard_map/ppermute | solution.py:218
  24.3 0.6 %shard_map.90 = (bf16[640,128]{1,0:T(8,128)(2,1)S(1)}, bf16[512,128]{1,0:T(8,128)(2,1)S(1)}, bf16[640,128]{1,0:T(8,128)(2,1)S(1)}, bf16[512,128]{1,0:T(8,128)(2,1)S(1)}) custom-call(s32[1,1024]{1,0:T(1,128)S(4)} %get-tuple-element.19.order, bf16[32,128,128]{2,1,0:T(8,128)(2,1)S(1)} %get-tuple-element.22.grads, ...), custom_call_target="tpu_custom_call" | custom-call | flops 1073741824 | bytes 8388608 | tf_op jit(solution)/shard_map/pallas_call | solution.py:273
  25.0 1.0 %collective-permute-start.11 = (bf16[640,128]{1,0:T(8,128)(2,1)S(1)}, bf16[640,128]{1,0:T(8,128)(2,1)S(1)}, u32[]{:S(2)}, u32[]{:S(2)}) collective-permute-start(bf16[640,128]{1,0:T(8,128)(2,1)S(1)} %get-tuple-element.28), channel_id=1, source_target_pairs={{0,48},{16,0},{32,16},{48,32},{1,17},{17,33},{33,49},{49,1},{2,50}... | collective-permute-start | bytes 491528 | tf_op jit(solution)/shard_map/ppermute | solution.py:218
  25.9 1.8 %collective-permute-start.9 = (bf16[640,128]{1,0:T(8,128)(2,1)S(1)}, bf16[640,128]{1,0:T(8,128)(2,1)S(1)}, u32[]{:S(2)}, u32[]{:S(2)}) collective-permute-start(bf16[640,128]{1,0:T(8,128)(2,1)S(1)} %get-tuple-element.24.after), channel_id=1, source_target_pairs={{0,16},{16,32},{32,48},{48,0},{1,49},{17,1},{33,17},{49,33},{2,18}... | collective-permute-start | bytes 491528 | tf_op jit(solution)/shard_map/ppermute | solution.py:218
  27.7 1.4 %collective-permute-start.13 = (bf16[512,128]{1,0:T(8,128)(2,1)S(1)}, bf16[512,128]{1,0:T(8,128)(2,1)S(1)}, u32[]{:S(2)}, u32[]{:S(2)}) collective-permute-start(bf16[512,128]{1,0:T(8,128)(2,1)S(1)} %get-tuple-element.31), channel_id=1, source_target_pairs={{0,48},{16,0},{32,16},{48,32},{1,17},{17,33},{33,49},{49,1},{2,50}... | collective-permute-start | bytes 393224 | tf_op jit(solution)/shard_map/ppermute | solution.py:218
  29.2 0.6 %shard_map.91 = (f32[512,128]{1,0:T(8,128)S(1)}, f32[512,128]{1,0:T(8,128)S(1)}) custom-call(s32[1,1024]{1,0:T(1,128)S(4)} %get-tuple-element.19.order, bf16[32,128,128]{2,1,0:T(8,128)(2,1)S(1)} %get-tuple-element.22.grads, bf16[256,128,128]{2,1,0:T(8,128)(2,1)S(1)} %get-tuple-element.21.refs_9_.tiles, bf16[640,128]{1,0:T(8,128)(2,1)S(1)} %get-tuple-element.24.after), custom_call_target="tpu_custom_call" | custom-call | flops 1073741824 | bytes 8388608 | tf_op jit(solution)/shard_map/pallas_call | solution.py:281
  29.7 6.3 %collective-permute-done.11.r3 = bf16[640,128]{1,0:T(8,128)(2,1)S(1)} collective-permute-done((bf16[640,128]{1,0:T(8,128)(2,1)S(1)}, bf16[640,128]{1,0:T(8,128)(2,1)S(1)}, u32[]{:S(2)}, u32[]{:S(2)}) %collective-permute-start.11) | collective-permute-done | bytes 163872 | tf_op jit(solution)/shard_map/ppermute | solution.py:218
  36.0 0.1 shard_map.92
  36.1 7.0 %collective-permute-start.15 = (bf16[384,128]{1,0:T(8,128)(2,1)S(1)}, bf16[384,128]{1,0:T(8,128)(2,1)S(1)}, u32[]{:S(2)}, u32[]{:S(2)}) collective-permute-start(bf16[384,128]{1,0:T(8,128)(2,1)S(1)} %get-tuple-element.34), channel_id=1, source_target_pairs={{0,128},{64,192},{128,0},{192,64},{1,129},{65,193},{129,1},{193,65... | collective-permute-start | bytes 294920 | tf_op jit(solution)/shard_map/ppermute | solution.py:218
  43.0 1.7 %collective-permute-start.16 = (bf16[384,128]{1,0:T(8,128)(2,1)S(1)}, bf16[384,128]{1,0:T(8,128)(2,1)S(1)}, u32[]{:S(2)}, u32[]{:S(2)}) collective-permute-start(bf16[384,128]{1,0:T(8,128)(2,1)S(1)} %get-tuple-element.35), channel_id=1, source_target_pairs={{0,192},{64,0},{128,64},{192,128},{1,65},{65,129},{129,193},{193,1... | collective-permute-start | bytes 294920 | tf_op jit(solution)/shard_map/ppermute | solution.py:218
  44.8 1.9 %collective-permute-start.14 = (bf16[384,128]{1,0:T(8,128)(2,1)S(1)}, bf16[384,128]{1,0:T(8,128)(2,1)S(1)}, u32[]{:S(2)}, u32[]{:S(2)}) collective-permute-start(bf16[384,128]{1,0:T(8,128)(2,1)S(1)} %get-tuple-element.33), channel_id=1, source_target_pairs={{0,64},{64,128},{128,192},{192,0},{1,193},{65,1},{129,65},{193,129... | collective-permute-start | bytes 294920 | tf_op jit(solution)/shard_map/ppermute | solution.py:218
  46.8 3.0 %collective-permute-done.16.r3 = bf16[384,128]{1,0:T(8,128)(2,1)S(1)} collective-permute-done((bf16[384,128]{1,0:T(8,128)(2,1)S(1)}, bf16[384,128]{1,0:T(8,128)(2,1)S(1)}, u32[]{:S(2)}, u32[]{:S(2)}) %collective-permute-start.16) | collective-permute-done | bytes 98336 | tf_op jit(solution)/shard_map/ppermute | solution.py:218
  49.8 3.4 %collective-permute-done.14.r1 = bf16[384,128]{1,0:T(8,128)(2,1)S(1)} collective-permute-done((bf16[384,128]{1,0:T(8,128)(2,1)S(1)}, bf16[384,128]{1,0:T(8,128)(2,1)S(1)}, u32[]{:S(2)}, u32[]{:S(2)}) %collective-permute-start.14) | collective-permute-done | bytes 98336 | tf_op jit(solution)/shard_map/ppermute | solution.py:218
  53.2 0.7 %shard_map.94 = (bf16[256,128]{1,0:T(8,128)(2,1)}, f32[128,128]{1,0:T(8,128)}) custom-call(f32[256,128]{1,0:T(8,128)S(1)} %get-tuple-element.32.keep, bf16[128,128]{1,0:T(8,128)(2,1)S(1)} %get-tuple-element.29.weight_y, bf16[384,128]{1,0:T(8,128)(2,1)S(1)} %collective-permute-done.14.r1, bf16[384,128]{1,0:T(8,128)(2,1)S(1)} %collective-permute-done.15.r2, ...), custom_call_target="tpu_custom_call" | custom-call | tf_op jit(solution)/shard_map/pallas_call | solution.py:302
  (13 shorter events, 0.1 us)
Async XLA Ops:
  1.8 4.3 %collective-permute-start = (bf16[256,256]{1,0:T(8,128)(2,1)S(1)}, bf16[256,256]{1,0:T(8,128)(2,1)S(1)}, u32[]{:S(2)}, u32[]{:S(2)}) collective-permute-start(bf16[256,256]{1,0:T(8,128)(2,1)S(1)} %shard_map.87.own), channel_id=1, source_target_pairs={{0,1},{1,0},{2,3},{3,2},{4,5},{5,4},{6,7},{7,6},{8,9},{9,8},{10,11... | collective-permute-start | bytes 393224 | tf_op jit(solution)/shard_map/ppermute | solution.py:240
  6.7 9.9 %collective-permute-start.4 = (bf16[320,256]{1,0:T(8,128)(2,1)S(1)}, bf16[320,256]{1,0:T(8,128)(2,1)S(1)}, u32[]{:S(2)}, u32[]{:S(2)}) collective-permute-start(bf16[320,256]{1,0:T(8,128)(2,1)S(1)} %shard_map.88.refs_0_), channel_id=1, source_target_pairs={{0,6},{1,11},{2,0},{3,13},{4,2},{5,15},{6,4},{7,9},{8,14},{9,3},{1... | collective-permute-start | bytes 491528 | tf_op jit(solution)/shard_map/ppermute | solution.py:255
  7.6 9.1 %collective-permute-start.3 = (bf16[320,256]{1,0:T(8,128)(2,1)S(1)}, bf16[320,256]{1,0:T(8,128)(2,1)S(1)}, u32[]{:S(2)}, u32[]{:S(2)}) collective-permute-start(bf16[320,256]{1,0:T(8,128)(2,1)S(1)} %shard_map.88.refs_0_), channel_id=1, source_target_pairs={{0,4},{1,13},{2,6},{3,15},{4,0},{5,9},{6,2},{7,11},{8,12},{9,5},{1... | collective-permute-start | bytes 491528 | tf_op jit(solution)/shard_map/ppermute | solution.py:255
  9.6 7.8 %collective-permute-start.2 = (bf16[320,256]{1,0:T(8,128)(2,1)S(1)}, bf16[320,256]{1,0:T(8,128)(2,1)S(1)}, u32[]{:S(2)}, u32[]{:S(2)}) collective-permute-start(bf16[320,256]{1,0:T(8,128)(2,1)S(1)} %shard_map.88.refs_0_), channel_id=1, source_target_pairs={{0,2},{1,15},{2,4},{3,9},{4,6},{5,11},{6,0},{7,13},{8,10},{9,7},{1... | collective-permute-start | bytes 491528 | tf_op jit(solution)/shard_map/ppermute | solution.py:255
  12.1 6.9 %collective-permute-start.1 = (bf16[320,256]{1,0:T(8,128)(2,1)S(1)}, bf16[320,256]{1,0:T(8,128)(2,1)S(1)}, u32[]{:S(2)}, u32[]{:S(2)}) collective-permute-start(bf16[320,256]{1,0:T(8,128)(2,1)S(1)} %shard_map.88.refs_0_), channel_id=1, source_target_pairs={{1,9},{3,11},{5,13},{7,15},{9,1},{11,3},{13,5},{15,7},{17,25},{19,... | collective-permute-start | bytes 491528 | tf_op jit(solution)/shard_map/ppermute | solution.py:255
  16.6 2.9 %collective-permute-start.7 = (bf16[320,256]{1,0:T(8,128)(2,1)S(1)}, bf16[320,256]{1,0:T(8,128)(2,1)S(1)}, u32[]{:S(2)}, u32[]{:S(2)}) collective-permute-start(bf16[320,256]{1,0:T(8,128)(2,1)S(1)} %collective-permute-done.3.refs_3_), channel_id=1, source_target_pairs={{0,1},{1,0},{2,3},{3,2},{4,5},{5,4},{6,7},{7,6},{8,9},{9,8},{10,11... | collective-permute-start | bytes 491528 | tf_op jit(solution)/shard_map/ppermute | solution.py:261
  17.3 2.7 %collective-permute-start.6 = (bf16[320,256]{1,0:T(8,128)(2,1)S(1)}, bf16[320,256]{1,0:T(8,128)(2,1)S(1)}, u32[]{:S(2)}, u32[]{:S(2)}) collective-permute-start(bf16[320,256]{1,0:T(8,128)(2,1)S(1)} %collective-permute-done.2.refs_2_), channel_id=1, source_target_pairs={{0,1},{1,0},{2,3},{3,2},{4,5},{5,4},{6,7},{7,6},{8,9},{9,8},{10,11... | collective-permute-start | bytes 491528 | tf_op jit(solution)/shard_map/ppermute | solution.py:261
  19.0 1.4 %collective-permute-start.5 = (bf16[320,256]{1,0:T(8,128)(2,1)S(1)}, bf16[320,256]{1,0:T(8,128)(2,1)S(1)}, u32[]{:S(2)}, u32[]{:S(2)}) collective-permute-start(bf16[320,256]{1,0:T(8,128)(2,1)S(1)} %collective-permute-done.1.refs_1_), channel_id=1, source_target_pairs={{0,1},{1,0},{2,3},{3,2},{4,5},{5,4},{6,7},{7,6},{8,9},{9,8},{10,11... | collective-permute-start | bytes 491528 | tf_op jit(solution)/shard_map/ppermute | solution.py:261
  19.0 1.6 %collective-permute-start.8 = (bf16[320,256]{1,0:T(8,128)(2,1)S(1)}, bf16[320,256]{1,0:T(8,128)(2,1)S(1)}, u32[]{:S(2)}, u32[]{:S(2)}) collective-permute-start(bf16[320,256]{1,0:T(8,128)(2,1)S(1)} %collective-permute-done.4.refs_4_), channel_id=1, source_target_pairs={{0,1},{1,0},{2,3},{3,2},{4,5},{5,4},{6,7},{7,6},{8,9},{9,8},{10,11... | collective-permute-start | bytes 491528 | tf_op jit(solution)/shard_map/ppermute | solution.py:261
  22.0 14.0 %collective-permute-start.10 = (bf16[1152,128]{1,0:T(8,128)(2,1)S(1)}, bf16[1152,128]{1,0:T(8,128)(2,1)S(1)}, u32[]{:S(2)}, u32[]{:S(2)}) collective-permute-start(bf16[1152,128]{1,0:T(8,128)(2,1)S(1)} %get-tuple-element.27), channel_id=1, source_target_pairs={{0,32},{16,48},{32,0},{48,16},{1,33},{17,49},{33,1},{49,17},{2,34}... | collective-permute-start | bytes 884744 | tf_op jit(solution)/shard_map/ppermute | solution.py:218
  25.0 11.0 %collective-permute-start.11 = (bf16[640,128]{1,0:T(8,128)(2,1)S(1)}, bf16[640,128]{1,0:T(8,128)(2,1)S(1)}, u32[]{:S(2)}, u32[]{:S(2)}) collective-permute-start(bf16[640,128]{1,0:T(8,128)(2,1)S(1)} %get-tuple-element.28), channel_id=1, source_target_pairs={{0,48},{16,0},{32,16},{48,32},{1,17},{17,33},{33,49},{49,1},{2,50}... | collective-permute-start | bytes 491528 | tf_op jit(solution)/shard_map/ppermute | solution.py:218
  25.9 10.1 %collective-permute-start.9 = (bf16[640,128]{1,0:T(8,128)(2,1)S(1)}, bf16[640,128]{1,0:T(8,128)(2,1)S(1)}, u32[]{:S(2)}, u32[]{:S(2)}) collective-permute-start(bf16[640,128]{1,0:T(8,128)(2,1)S(1)} %get-tuple-element.24.after), channel_id=1, source_target_pairs={{0,16},{16,32},{32,48},{48,0},{1,49},{17,1},{33,17},{49,33},{2,18}... | collective-permute-start | bytes 491528 | tf_op jit(solution)/shard_map/ppermute | solution.py:218
  27.7 17.1 %collective-permute-start.12 = (bf16[512,128]{1,0:T(8,128)(2,1)S(1)}, bf16[512,128]{1,0:T(8,128)(2,1)S(1)}, u32[]{:S(2)}, u32[]{:S(2)}) collective-permute-start(bf16[512,128]{1,0:T(8,128)(2,1)S(1)} %get-tuple-element.30), channel_id=1, source_target_pairs={{0,16},{16,32},{32,48},{48,0},{1,49},{17,1},{33,17},{49,33},{2,18}... | collective-permute-start | bytes 393224 | tf_op jit(solution)/shard_map/ppermute | solution.py:218
  27.7 17.0 %collective-permute-start.13 = (bf16[512,128]{1,0:T(8,128)(2,1)S(1)}, bf16[512,128]{1,0:T(8,128)(2,1)S(1)}, u32[]{:S(2)}, u32[]{:S(2)}) collective-permute-start(bf16[512,128]{1,0:T(8,128)(2,1)S(1)} %get-tuple-element.31), channel_id=1, source_target_pairs={{0,48},{16,0},{32,16},{48,32},{1,17},{17,33},{33,49},{49,1},{2,50}... | collective-permute-start | bytes 393224 | tf_op jit(solution)/shard_map/ppermute | solution.py:218
  36.1 10.7 %collective-permute-start.15 = (bf16[384,128]{1,0:T(8,128)(2,1)S(1)}, bf16[384,128]{1,0:T(8,128)(2,1)S(1)}, u32[]{:S(2)}, u32[]{:S(2)}) collective-permute-start(bf16[384,128]{1,0:T(8,128)(2,1)S(1)} %get-tuple-element.34), channel_id=1, source_target_pairs={{0,128},{64,192},{128,0},{192,64},{1,129},{65,193},{129,1},{193,65... | collective-permute-start | bytes 294920 | tf_op jit(solution)/shard_map/ppermute | solution.py:218
  43.0 6.8 %collective-permute-start.16 = (bf16[384,128]{1,0:T(8,128)(2,1)S(1)}, bf16[384,128]{1,0:T(8,128)(2,1)S(1)}, u32[]{:S(2)}, u32[]{:S(2)}) collective-permute-start(bf16[384,128]{1,0:T(8,128)(2,1)S(1)} %get-tuple-element.35), channel_id=1, source_target_pairs={{0,192},{64,0},{128,64},{192,128},{1,65},{65,129},{129,193},{193,1... | collective-permute-start | bytes 294920 | tf_op jit(solution)/shard_map/ppermute | solution.py:218
  44.8 8.4 %collective-permute-start.14 = (bf16[384,128]{1,0:T(8,128)(2,1)S(1)}, bf16[384,128]{1,0:T(8,128)(2,1)S(1)}, u32[]{:S(2)}, u32[]{:S(2)}) collective-permute-start(bf16[384,128]{1,0:T(8,128)(2,1)S(1)} %get-tuple-element.33), channel_id=1, source_target_pairs={{0,64},{64,128},{128,192},{192,0},{1,193},{65,1},{129,65},{193,129... | collective-permute-start | bytes 294920 | tf_op jit(solution)/shard_map/ppermute | solution.py:218
where the time goes:
time: 54.4 us; the launch traced here: 54 us
  starting transfers between devices  30.7 us (56%)
  waiting for transfers between devices  14.7 us (27%)
  Pallas kernels  6.11 us (11%)
  between operations  1.38 us (3%)
  other arithmetic  0.94 us (2%)
    ppermute x8, starting transfers between devices, around(): return lax.ppermute(value, (axis, 'core'), pairs)  17.2 us
    ppermute x8, waiting for transfers between devices, around(): return lax.ppermute(value, (axis, 'core'), pairs)  12.7 us
    ppermute x4, starting transfers between devices, body(): got = [lax.ppermute(mine, COLS, chip_perm(k)) for k in range(4)]  7.32 us
    ppermute x1, starting transfers between devices, body(): lax.ppermute(local, 'core', swap)  3.33 us
    ppermute x4, starting transfers between devices, body(): swapped.append(lax.ppermute(ready, 'core', swap))  2.85 us
    pallas_call x1, Pallas kernels, body(): call(order_kernel, [pltpu.SMEM((1, PLACES), i32), pltpu.VMEM((SLOTS, T, T...  1.97 us
    pallas_call x1, Pallas kernels, body(): call(first_kernel, [struct(BLOCKS, T, T), struct(T, T), struct(9 * T, T)]...  1.33 us
    ppermute x4, waiting for transfers between devices, body(): swapped.append(lax.ppermute(ready, 'core', swap))  1.12 us
  transfers between devices with their start and end apart: 17, of which 7 were waited for; matrix products, arithmetic and copies ran while one was open for 0% of the time, Pallas kernels for 6%

commit v1 on v0

--- a/solution.py
+++ b/solution.py
@@ -119,9 +119,15 @@
             )
 
 
+def put(acc, first, early, late):
+    for i in range(4):
+        early[i * T : (i + 1) * T, :] = acc[first + i].astype(early.dtype)
+        late[i * T : (i + 1) * T, :] = acc[first + 4 + i].astype(late.dtype)
+
+
 def first_kernel(pos, order, *refs):
     mine, got, swapped = refs[0], refs[1:5], refs[5:9]
-    tiles, grads, weight_part, send, acc, parts = refs[9:]
+    tiles, grads, weight_part, early, late, acc, parts = refs[9:]
     zl, x, core = pos[2], pos[3], pos[4]
 
     arrived = [(got[k], core, k) for k in range(4)]
@@ -140,31 +146,26 @@
     weight_part[0:64, :] = rounded[:, 0:T]
     weight_part[64:T, :] = rounded[:, T : 2 * T]
     multiply(0, order, grads, tiles, acc)
-    for i in range(8):
-        send[i * T : (i + 1) * T, :] = acc[i].astype(bf16)
-    send[8 * T : 9 * T, :] = weight_part[...]
+    put(acc, 0, early, late)
+    early[4 * T : 5 * T, :] = weight_part[...]
 
 
 def second_kernel(order, grads, weight_part, tiles, early_1, late_1, early_3, late_3, acc):
     multiply(1, order, grads, tiles, acc)
     for first, early, late in ((0, early_1, late_1), (8, early_3, late_3)):
-        for i in range(4):
-            early[i * T : (i + 1) * T, :] = acc[first + i].astype(bf16)
-            late[i * T : (i + 1) * T, :] = acc[first + 4 + i].astype(bf16)
+        put(acc, first, early, late)
         early[4 * T : 5 * T, :] = weight_part[...]
 
 
 def third_kernel(order, grads, tiles, after, early, late, acc):
     del after
     multiply(2, order, grads, tiles, acc)
-    for i in range(4):
-        early[i * T : (i + 1) * T, :] = acc[i]
-        late[i * T : (i + 1) * T, :] = acc[4 + i]
+    put(acc, 0, early, late)
 
 
 def early_kernel(own, weight_part, r1, r2, r3, send_2, send_3, weight_y):
-    parts = [r1[4 * T : 5 * T, :], r2[8 * T : 9 * T, :], r3[4 * T : 5 * T, :]]
-    rounded = ring_sum(weight_part[...].astype(f32), [p.astype(f32) for p in parts]).astype(bf16)
+    parts = [r[4 * T : 5 * T, :].astype(f32) for r in (r1, r2, r3)]
+    rounded = ring_sum(weight_part[...].astype(f32), parts).astype(bf16)
     weight_y[...] = rounded
     for i, out in enumerate((send_2, send_3)):
         rows = pl.ds(i * 2 * T, 2 * T)
@@ -178,8 +179,8 @@
 def late_kernel(own, weight_y, r1, r2, r3, keep, send_1):
     for i, out in enumerate((keep, send_1)):
         rows = pl.ds(i * 2 * T, 2 * T)
-        total = own[rows, :] + r2[(i + 2) * 2 * T : (i + 3) * 2 * T, :].astype(f32)
-        for r in (r1, r3):
+        total = own[rows, :]
+        for r in (r1, r2, r3):
             total += r[rows, :].astype(f32)
         out[0 : 2 * T, :] = total.astype(out.dtype)
     send_1[2 * T : 3 * T, :] = weight_y[...]
@@ -263,9 +264,9 @@
         flops=share * SLOTS * 2 * T**3, bytes_accessed=share * SLOTS * T * T * 2, transcendentals=0
     )
     early, late, onward = struct(5 * T, T), struct(4 * T, T), struct(3 * T, T)
-    grads, weight_part, send_2 = call(
+    grads, weight_part, early_2, late_2 = call(
         first_kernel,
-        [struct(BLOCKS, T, T), struct(T, T), struct(9 * T, T)],
+        [struct(BLOCKS, T, T), struct(T, T), early, late],
         [smem] * 2 + [vmem] * 10,
         [pltpu.VMEM((9, T, T), f32), pltpu.VMEM((8, 64, 2 * T), bf16)],
         cost(1),
@@ -277,7 +278,6 @@
         [pltpu.VMEM((17, T, T), f32)],
         cost(1),
     )(order, grads, weight_part, held)
-    got_2 = around("y", send_2, 2)
     own_early, own_late = call(
         third_kernel,
         [struct(4 * T, T, dtype=f32)] * 2,
@@ -285,8 +285,8 @@
         [pltpu.VMEM((9, T, T), f32)],
         cost(1),
     )(order, grads, held, early_1)
-    got_early = [around("y", early_1, 1), got_2, around("y", early_3, 3)]
-    got_late = [around("y", late_1, 1), got_2, around("y", late_3, 3)]
+    got_early = [around("y", v, d) for d, v in ((1, early_1), (2, early_2), (3, early_3))]
+    got_late = [around("y", v, d) for d, v in ((1, late_1), (2, late_2), (3, late_3))]
     send_2, send_3, weight_y = call(
         early_kernel, [onward, onward, struct(T, T)], [vmem] * 5, cost=cost(10)
     )(own_early, weight_part, *got_early)

time: 54.4 us -> 51.9 us (0.954)
  waiting for transfers between devices: 14.7 us -> 11.3 us
  starting transfers between devices: 30.7 us -> 31.9 us
    ppermute x8 -> x9, waiting for transfers between devices: 12.7 us -> 9.32 us  [around(): return lax.ppermute(value, (axis, 'core'), pairs)]
    ppermute x8 -> x9, starting transfers between devices: 17.2 us -> 18.5 us  [around(): return lax.ppermute(value, (axis, 'core'), pairs)]
  transfers between devices with their start and end apart: 17 -> 18, of which waited for: 7 -> 8; matrix products, arithmetic and copies ran while one was open for 0% -> 0% of each run, Pallas kernels for 6% -> 7%
where the time goes in v1:
time: 51.9 us
  starting transfers between devices  31.9 us (61%)
  waiting for transfers between devices  11.3 us (22%)
  Pallas kernels  6.24 us (12%)
  between operations  1.39 us (3%)
  other arithmetic  0.94 us (2%)
    ppermute x9, starting transfers between devices, around(): return lax.ppermute(value, (axis, 'core'), pairs)  18.5 us
    ppermute x9, waiting for transfers between devices, around(): return lax.ppermute(value, (axis, 'core'), pairs)  9.32 us
    ppermute x4, starting transfers between devices, body(): got = [lax.ppermute(mine, COLS, chip_perm(k)) for k in range(4)]  7.32 us
    ppermute x1, starting transfers between devices, body(): lax.ppermute(local, 'core', swap)  3.33 us
    ppermute x4, starting transfers between devices, body(): swapped.append(lax.ppermute(ready, 'core', swap))  2.73 us
    pallas_call x1, Pallas kernels, body(): call(order_kernel, [pltpu.SMEM((1, PLACES), i32), pltpu.VMEM((SLOTS, T, T...  2.09 us
    pallas_call x1, Pallas kernels, body(): call(first_kernel, [struct(BLOCKS, T, T), struct(T, T), early, late], [sm...  1.33 us
    ppermute x4, waiting for transfers between devices, body(): swapped.append(lax.ppermute(ready, 'core', swap))  1.12 us
  transfers between devices with their start and end apart: 18, of which 8 were waited for; matrix products, arithmetic and copies ran while one was open for 0% of the time, Pallas kernels for 7%

profile of v1, /device:TPU:1, one launch (start us, length us, event | category | flops | bytes accessed | tf_op | source)
XLA Modules:
  0.0 51.9 jit_solution(11301247738261791609)
XLA Ops:
  0.6 0.9 %pad_maximum_fusion.inputs = bf16[896,128]{1,0:T(8,128)(2,1)S(1)} fusion(bf16[128,128]{1,0:T(8,128)(2,1)} %param.10, bf16[256,128]{1,0:T(8,128)(2,1)} %param.9, bf16[256,128]{1,0:T(8,128)(2,1)} %param.8, bf16[256,128]{1,0:T(8,128)(2,1)} %param.7), kind=kLoop, calls=%fused_computation | loop fusion | flops 917504 | bytes 458752 | tf_op jit(solution)/shard_map/concatenate | solution.py:237
  1.6 0.2 shard_map.87.own
  1.8 3.3 %collective-permute-start = (bf16[256,256]{1,0:T(8,128)(2,1)S(1)}, bf16[256,256]{1,0:T(8,128)(2,1)S(1)}, u32[]{:S(2)}, u32[]{:S(2)}) collective-permute-start(bf16[256,256]{1,0:T(8,128)(2,1)S(1)} %shard_map.87.own), channel_id=1, source_target_pairs={{0,1},{1,0},{2,3},{3,2},{4,5},{5,4},{6,7},{7,6},{8,9},{9,8},{10,11... | collective-permute-start | bytes 393224 | tf_op jit(solution)/shard_map/ppermute | solution.py:241
  5.2 0.9 %collective-permute-done.other = bf16[256,256]{1,0:T(8,128)(2,1)S(1)} collective-permute-done((bf16[256,256]{1,0:T(8,128)(2,1)S(1)}, bf16[256,256]{1,0:T(8,128)(2,1)S(1)}, u32[]{:S(2)}, u32[]{:S(2)}) %collective-permute-start) | collective-permute-done | bytes 131104 | tf_op jit(solution)/shard_map/ppermute | solution.py:241
  6.1 0.6 %shard_map.88.refs_0_ = bf16[320,256]{1,0:T(8,128)(2,1)S(1)} custom-call(s32[5]{0:T(128)S(1)} %stack.23.pos, bf16[256,256]{1,0:T(8,128)(2,1)S(1)} %shard_map.87.own, bf16[256,256]{1,0:T(8,128)(2,1)S(1)} %collective-permute-done.other), custom_call_target="tpu_custom_call" | custom-call | tf_op jit(solution)/shard_map/pallas_call | solution.py:240
  6.7 0.9 %collective-permute-start.4 = (bf16[320,256]{1,0:T(8,128)(2,1)S(1)}, bf16[320,256]{1,0:T(8,128)(2,1)S(1)}, u32[]{:S(2)}, u32[]{:S(2)}) collective-permute-start(bf16[320,256]{1,0:T(8,128)(2,1)S(1)} %shard_map.88.refs_0_), channel_id=1, source_target_pairs={{0,6},{1,11},{2,0},{3,13},{4,2},{5,15},{6,4},{7,9},{8,14},{9,3},{1... | collective-permute-start | bytes 491528 | tf_op jit(solution)/shard_map/ppermute | solution.py:256
  7.6 2.0 %collective-permute-start.3 = (bf16[320,256]{1,0:T(8,128)(2,1)S(1)}, bf16[320,256]{1,0:T(8,128)(2,1)S(1)}, u32[]{:S(2)}, u32[]{:S(2)}) collective-permute-start(bf16[320,256]{1,0:T(8,128)(2,1)S(1)} %shard_map.88.refs_0_), channel_id=1, source_target_pairs={{0,4},{1,13},{2,6},{3,15},{4,0},{5,9},{6,2},{7,11},{8,12},{9,5},{1... | collective-permute-start | bytes 491528 | tf_op jit(solution)/shard_map/ppermute | solution.py:256
  9.6 2.5 %collective-permute-start.2 = (bf16[320,256]{1,0:T(8,128)(2,1)S(1)}, bf16[320,256]{1,0:T(8,128)(2,1)S(1)}, u32[]{:S(2)}, u32[]{:S(2)}) collective-permute-start(bf16[320,256]{1,0:T(8,128)(2,1)S(1)} %shard_map.88.refs_0_), channel_id=1, source_target_pairs={{0,2},{1,15},{2,4},{3,9},{4,6},{5,11},{6,0},{7,13},{8,10},{9,7},{1... | collective-permute-start | bytes 491528 | tf_op jit(solution)/shard_map/ppermute | solution.py:256
  12.1 1.9 %collective-permute-start.1 = (bf16[320,256]{1,0:T(8,128)(2,1)S(1)}, bf16[320,256]{1,0:T(8,128)(2,1)S(1)}, u32[]{:S(2)}, u32[]{:S(2)}) collective-permute-start(bf16[320,256]{1,0:T(8,128)(2,1)S(1)} %shard_map.88.refs_0_), channel_id=1, source_target_pairs={{1,9},{3,11},{5,13},{7,15},{9,1},{11,3},{13,5},{15,7},{17,25},{19,... | collective-permute-start | bytes 491528 | tf_op jit(solution)/shard_map/ppermute | solution.py:256
  14.7 2.1 %shard_map.86 = (s32[1,1024]{1,0:T(1,128)S(4)}, bf16[256,128,128]{2,1,0:T(8,128)(2,1)S(1)}) custom-call(s32[5]{0:T(128)S(1)} %stack.23.pos, s32[1]{0:T(128)} %bitcast.8.count_ref, s32[2,256]{1,0:T(2,128)} %bitcast.10, bf16[256,128,128]{2,1,0:T(8,128)(2,1)} %bitcast.9), custom_call_target="tpu_custom_call" | custom-call | bytes 16777216 | tf_op jit(solution)/shard_map/pallas_call | solution.py:243
  16.8 0.6 %collective-permute-start.7 = (bf16[320,256]{1,0:T(8,128)(2,1)S(1)}, bf16[320,256]{1,0:T(8,128)(2,1)S(1)}, u32[]{:S(2)}, u32[]{:S(2)}) collective-permute-start(bf16[320,256]{1,0:T(8,128)(2,1)S(1)} %collective-permute-done.3.refs_3_), channel_id=1, source_target_pairs={{0,1},{1,0},{2,3},{3,2},{4,5},{5,4},{6,7},{7,6},{8,9},{9,8},{10,11... | collective-permute-start | bytes 491528 | tf_op jit(solution)/shard_map/ppermute | solution.py:262
  17.3 1.6 %collective-permute-start.6 = (bf16[320,256]{1,0:T(8,128)(2,1)S(1)}, bf16[320,256]{1,0:T(8,128)(2,1)S(1)}, u32[]{:S(2)}, u32[]{:S(2)}) collective-permute-start(bf16[320,256]{1,0:T(8,128)(2,1)S(1)} %collective-permute-done.2.refs_2_), channel_id=1, source_target_pairs={{0,1},{1,0},{2,3},{3,2},{4,5},{5,4},{6,7},{7,6},{8,9},{9,8},{10,11... | collective-permute-start | bytes 491528 | tf_op jit(solution)/shard_map/ppermute | solution.py:262
  19.0 0.5 collective-permute-start.8
  19.5 0.5 collective-permute-done.6.refs_6_
  20.0 0.4 collective-permute-done.5.refs_5_
  20.4 0.2 collective-permute-done.8.refs_8_
  20.6 1.3 %shard_map.89 = (bf16[32,128,128]{2,1,0:T(8,128)(2,1)S(1)}, bf16[128,128]{1,0:T(8,128)(2,1)S(1)}, bf16[640,128]{1,0:T(8,128)(2,1)S(1)}, bf16[512,128]{1,0:T(8,128)(2,1)S(1)}) custom-call(s32[5]{0:T(128)S(1)} %stack.23.pos, s32[1,1024]{1,0:T(1,128)S(4)} %get-tuple-element.20.order, bf16[320,256]{1,0:T(8,128)(2,1)S(1)} %shard_map.88.refs_0_, ...), custom_call_target="tpu_custom_call" | custom-call | flops 1073741824 | bytes 8388608 | tf_op jit(solution)/shard_map/pallas_call | solution.py:267
  22.0 2.4 %collective-permute-start.10 = (bf16[640,128]{1,0:T(8,128)(2,1)S(1)}, bf16[640,128]{1,0:T(8,128)(2,1)S(1)}, u32[]{:S(2)}, u32[]{:S(2)}) collective-permute-start(bf16[640,128]{1,0:T(8,128)(2,1)S(1)} %get-tuple-element.28), channel_id=1, source_target_pairs={{0,32},{16,48},{32,0},{48,16},{1,33},{17,49},{33,1},{49,17},{2,34}... | collective-permute-start | bytes 491528 | tf_op jit(solution)/shard_map/ppermute | solution.py:219
  24.3 0.6 %shard_map.90 = (bf16[640,128]{1,0:T(8,128)(2,1)S(1)}, bf16[512,128]{1,0:T(8,128)(2,1)S(1)}, bf16[640,128]{1,0:T(8,128)(2,1)S(1)}, bf16[512,128]{1,0:T(8,128)(2,1)S(1)}) custom-call(s32[1,1024]{1,0:T(1,128)S(4)} %get-tuple-element.20.order, bf16[32,128,128]{2,1,0:T(8,128)(2,1)S(1)} %get-tuple-element.23.grads, ...), custom_call_target="tpu_custom_call" | custom-call | flops 1073741824 | bytes 8388608 | tf_op jit(solution)/shard_map/pallas_call | solution.py:274
  25.0 0.7 %collective-permute-start.11 = (bf16[640,128]{1,0:T(8,128)(2,1)S(1)}, bf16[640,128]{1,0:T(8,128)(2,1)S(1)}, u32[]{:S(2)}, u32[]{:S(2)}) collective-permute-start(bf16[640,128]{1,0:T(8,128)(2,1)S(1)} %get-tuple-element.29), channel_id=1, source_target_pairs={{0,48},{16,0},{32,16},{48,32},{1,17},{17,33},{33,49},{49,1},{2,50}... | collective-permute-start | bytes 491528 | tf_op jit(solution)/shard_map/ppermute | solution.py:219
  25.7 2.0 %collective-permute-start.9 = (bf16[640,128]{1,0:T(8,128)(2,1)S(1)}, bf16[640,128]{1,0:T(8,128)(2,1)S(1)}, u32[]{:S(2)}, u32[]{:S(2)}) collective-permute-start(bf16[640,128]{1,0:T(8,128)(2,1)S(1)} %get-tuple-element.25.after), channel_id=1, source_target_pairs={{0,16},{16,32},{32,48},{48,0},{1,49},{17,1},{33,17},{49,33},{2,18}... | collective-permute-start | bytes 491528 | tf_op jit(solution)/shard_map/ppermute | solution.py:219
  27.7 0.2 collective-permute-start.13
  28.0 1.6 %collective-permute-start.12 = (bf16[512,128]{1,0:T(8,128)(2,1)S(1)}, bf16[512,128]{1,0:T(8,128)(2,1)S(1)}, u32[]{:S(2)}, u32[]{:S(2)}) collective-permute-start(bf16[512,128]{1,0:T(8,128)(2,1)S(1)} %get-tuple-element.31), channel_id=1, source_target_pairs={{0,16},{16,32},{32,48},{48,0},{1,49},{17,1},{33,17},{49,33},{2,18}... | collective-permute-start | bytes 393224 | tf_op jit(solution)/shard_map/ppermute | solution.py:219
  29.5 0.6 %shard_map.91 = (f32[512,128]{1,0:T(8,128)S(1)}, f32[512,128]{1,0:T(8,128)S(1)}) custom-call(s32[1,1024]{1,0:T(1,128)S(4)} %get-tuple-element.20.order, bf16[32,128,128]{2,1,0:T(8,128)(2,1)S(1)} %get-tuple-element.23.grads, bf16[256,128,128]{2,1,0:T(8,128)(2,1)S(1)} %get-tuple-element.22.refs_9_.tiles, bf16[640,128]{1,0:T(8,128)(2,1)S(1)} %get-tuple-element.25.after), custom_call_target="tpu_custom_call" | custom-call | flops 1073741824 | bytes 8388608 | tf_op jit(solution)/shard_map/pallas_call | solution.py:281
  30.2 1.8 %collective-permute-done.11.r3 = bf16[640,128]{1,0:T(8,128)(2,1)S(1)} collective-permute-done((bf16[640,128]{1,0:T(8,128)(2,1)S(1)}, bf16[640,128]{1,0:T(8,128)(2,1)S(1)}, u32[]{:S(2)}, u32[]{:S(2)}) %collective-permute-start.11) | collective-permute-done | bytes 163872 | tf_op jit(solution)/shard_map/ppermute | solution.py:219
  32.0 0.8 %collective-permute-done.9.r1 = bf16[640,128]{1,0:T(8,128)(2,1)S(1)} collective-permute-done((bf16[640,128]{1,0:T(8,128)(2,1)S(1)}, bf16[640,128]{1,0:T(8,128)(2,1)S(1)}, u32[]{:S(2)}, u32[]{:S(2)}) %collective-permute-start.9) | collective-permute-done | bytes 163872 | tf_op jit(solution)/shard_map/ppermute | solution.py:219
  32.9 6.7 %collective-permute-start.16 = (bf16[384,128]{1,0:T(8,128)(2,1)S(1)}, bf16[384,128]{1,0:T(8,128)(2,1)S(1)}, u32[]{:S(2)}, u32[]{:S(2)}) collective-permute-start(bf16[384,128]{1,0:T(8,128)(2,1)S(1)} %get-tuple-element.36), channel_id=1, source_target_pairs={{0,128},{64,192},{128,0},{192,64},{1,129},{65,193},{129,1},{193,65... | collective-permute-start | bytes 294920 | tf_op jit(solution)/shard_map/ppermute | solution.py:219
  39.5 1.1 %collective-permute-start.17 = (bf16[384,128]{1,0:T(8,128)(2,1)S(1)}, bf16[384,128]{1,0:T(8,128)(2,1)S(1)}, u32[]{:S(2)}, u32[]{:S(2)}) collective-permute-start(bf16[384,128]{1,0:T(8,128)(2,1)S(1)} %get-tuple-element.37), channel_id=1, source_target_pairs={{0,192},{64,0},{128,64},{192,128},{1,65},{65,129},{129,193},{193,1... | collective-permute-start | bytes 294920 | tf_op jit(solution)/shard_map/ppermute | solution.py:219
  40.8 3.7 %collective-permute-start.15 = (bf16[384,128]{1,0:T(8,128)(2,1)S(1)}, bf16[384,128]{1,0:T(8,128)(2,1)S(1)}, u32[]{:S(2)}, u32[]{:S(2)}) collective-permute-start(bf16[384,128]{1,0:T(8,128)(2,1)S(1)} %get-tuple-element.35), channel_id=1, source_target_pairs={{0,64},{64,128},{128,192},{192,0},{1,193},{65,1},{129,65},{193,129... | collective-permute-start | bytes 294920 | tf_op jit(solution)/shard_map/ppermute | solution.py:219
  44.5 3.4 %collective-permute-done.17.r3 = bf16[384,128]{1,0:T(8,128)(2,1)S(1)} collective-permute-done((bf16[384,128]{1,0:T(8,128)(2,1)S(1)}, bf16[384,128]{1,0:T(8,128)(2,1)S(1)}, u32[]{:S(2)}, u32[]{:S(2)}) %collective-permute-start.17) | collective-permute-done | bytes 98336 | tf_op jit(solution)/shard_map/ppermute | solution.py:219
  47.9 3.3 %collective-permute-done.15.r1 = bf16[384,128]{1,0:T(8,128)(2,1)S(1)} collective-permute-done((bf16[384,128]{1,0:T(8,128)(2,1)S(1)}, bf16[384,128]{1,0:T(8,128)(2,1)S(1)}, u32[]{:S(2)}, u32[]{:S(2)}) %collective-permute-start.15) | collective-permute-done | bytes 98336 | tf_op jit(solution)/shard_map/ppermute | solution.py:219
  51.2 0.7 %shard_map.94 = (bf16[256,128]{1,0:T(8,128)(2,1)}, f32[128,128]{1,0:T(8,128)}) custom-call(f32[256,128]{1,0:T(8,128)S(1)} %get-tuple-element.34.keep, bf16[128,128]{1,0:T(8,128)(2,1)S(1)} %get-tuple-element.30.weight_y, bf16[384,128]{1,0:T(8,128)(2,1)S(1)} %collective-permute-done.15.r1, bf16[384,128]{1,0:T(8,128)(2,1)S(1)} %collective-permute-done.16.r2, ...), custom_call_target="tpu_custom_call" | custom-call | tf_op jit(solution)/shard_map/pallas_call | solution.py:302
  (15 shorter events, 0.3 us)
Async XLA Ops:
  1.8 4.3 %collective-permute-start = (bf16[256,256]{1,0:T(8,128)(2,1)S(1)}, bf16[256,256]{1,0:T(8,128)(2,1)S(1)}, u32[]{:S(2)}, u32[]{:S(2)}) collective-permute-start(bf16[256,256]{1,0:T(8,128)(2,1)S(1)} %shard_map.87.own), channel_id=1, source_target_pairs={{0,1},{1,0},{2,3},{3,2},{4,5},{5,4},{6,7},{7,6},{8,9},{9,8},{10,11... | collective-permute-start | bytes 393224 | tf_op jit(solution)/shard_map/ppermute | solution.py:241
  6.7 10.1 %collective-permute-start.4 = (bf16[320,256]{1,0:T(8,128)(2,1)S(1)}, bf16[320,256]{1,0:T(8,128)(2,1)S(1)}, u32[]{:S(2)}, u32[]{:S(2)}) collective-permute-start(bf16[320,256]{1,0:T(8,128)(2,1)S(1)} %shard_map.88.refs_0_), channel_id=1, source_target_pairs={{0,6},{1,11},{2,0},{3,13},{4,2},{5,15},{6,4},{7,9},{8,14},{9,3},{1... | collective-permute-start | bytes 491528 | tf_op jit(solution)/shard_map/ppermute | solution.py:256
  7.6 9.2 %collective-permute-start.3 = (bf16[320,256]{1,0:T(8,128)(2,1)S(1)}, bf16[320,256]{1,0:T(8,128)(2,1)S(1)}, u32[]{:S(2)}, u32[]{:S(2)}) collective-permute-start(bf16[320,256]{1,0:T(8,128)(2,1)S(1)} %shard_map.88.refs_0_), channel_id=1, source_target_pairs={{0,4},{1,13},{2,6},{3,15},{4,0},{5,9},{6,2},{7,11},{8,12},{9,5},{1... | collective-permute-start | bytes 491528 | tf_op jit(solution)/shard_map/ppermute | solution.py:256
  9.6 7.8 %collective-permute-start.2 = (bf16[320,256]{1,0:T(8,128)(2,1)S(1)}, bf16[320,256]{1,0:T(8,128)(2,1)S(1)}, u32[]{:S(2)}, u32[]{:S(2)}) collective-permute-start(bf16[320,256]{1,0:T(8,128)(2,1)S(1)} %shard_map.88.refs_0_), channel_id=1, source_target_pairs={{0,2},{1,15},{2,4},{3,9},{4,6},{5,11},{6,0},{7,13},{8,10},{9,7},{1... | collective-permute-start | bytes 491528 | tf_op jit(solution)/shard_map/ppermute | solution.py:256
  12.1 6.9 %collective-permute-start.1 = (bf16[320,256]{1,0:T(8,128)(2,1)S(1)}, bf16[320,256]{1,0:T(8,128)(2,1)S(1)}, u32[]{:S(2)}, u32[]{:S(2)}) collective-permute-start(bf16[320,256]{1,0:T(8,128)(2,1)S(1)} %shard_map.88.refs_0_), channel_id=1, source_target_pairs={{1,9},{3,11},{5,13},{7,15},{9,1},{11,3},{13,5},{15,7},{17,25},{19,... | collective-permute-start | bytes 491528 | tf_op jit(solution)/shard_map/ppermute | solution.py:256
  16.8 2.7 %collective-permute-start.7 = (bf16[320,256]{1,0:T(8,128)(2,1)S(1)}, bf16[320,256]{1,0:T(8,128)(2,1)S(1)}, u32[]{:S(2)}, u32[]{:S(2)}) collective-permute-start(bf16[320,256]{1,0:T(8,128)(2,1)S(1)} %collective-permute-done.3.refs_3_), channel_id=1, source_target_pairs={{0,1},{1,0},{2,3},{3,2},{4,5},{5,4},{6,7},{7,6},{8,9},{9,8},{10,11... | collective-permute-start | bytes 491528 | tf_op jit(solution)/shard_map/ppermute | solution.py:262
  17.3 2.7 %collective-permute-start.6 = (bf16[320,256]{1,0:T(8,128)(2,1)S(1)}, bf16[320,256]{1,0:T(8,128)(2,1)S(1)}, u32[]{:S(2)}, u32[]{:S(2)}) collective-permute-start(bf16[320,256]{1,0:T(8,128)(2,1)S(1)} %collective-permute-done.2.refs_2_), channel_id=1, source_target_pairs={{0,1},{1,0},{2,3},{3,2},{4,5},{5,4},{6,7},{7,6},{8,9},{9,8},{10,11... | collective-permute-start | bytes 491528 | tf_op jit(solution)/shard_map/ppermute | solution.py:262
  19.0 1.4 %collective-permute-start.5 = (bf16[320,256]{1,0:T(8,128)(2,1)S(1)}, bf16[320,256]{1,0:T(8,128)(2,1)S(1)}, u32[]{:S(2)}, u32[]{:S(2)}) collective-permute-start(bf16[320,256]{1,0:T(8,128)(2,1)S(1)} %collective-permute-done.1.refs_1_), channel_id=1, source_target_pairs={{0,1},{1,0},{2,3},{3,2},{4,5},{5,4},{6,7},{7,6},{8,9},{9,8},{10,11... | collective-permute-start | bytes 491528 | tf_op jit(solution)/shard_map/ppermute | solution.py:262
  19.0 1.6 %collective-permute-start.8 = (bf16[320,256]{1,0:T(8,128)(2,1)S(1)}, bf16[320,256]{1,0:T(8,128)(2,1)S(1)}, u32[]{:S(2)}, u32[]{:S(2)}) collective-permute-start(bf16[320,256]{1,0:T(8,128)(2,1)S(1)} %collective-permute-done.4.refs_4_), channel_id=1, source_target_pairs={{0,1},{1,0},{2,3},{3,2},{4,5},{5,4},{6,7},{7,6},{8,9},{9,8},{10,11... | collective-permute-start | bytes 491528 | tf_op jit(solution)/shard_map/ppermute | solution.py:262
  22.0 8.1 %collective-permute-start.10 = (bf16[640,128]{1,0:T(8,128)(2,1)S(1)}, bf16[640,128]{1,0:T(8,128)(2,1)S(1)}, u32[]{:S(2)}, u32[]{:S(2)}) collective-permute-start(bf16[640,128]{1,0:T(8,128)(2,1)S(1)} %get-tuple-element.28), channel_id=1, source_target_pairs={{0,32},{16,48},{32,0},{48,16},{1,33},{17,49},{33,1},{49,17},{2,34}... | collective-permute-start | bytes 491528 | tf_op jit(solution)/shard_map/ppermute | solution.py:219
  25.0 7.0 %collective-permute-start.11 = (bf16[640,128]{1,0:T(8,128)(2,1)S(1)}, bf16[640,128]{1,0:T(8,128)(2,1)S(1)}, u32[]{:S(2)}, u32[]{:S(2)}) collective-permute-start(bf16[640,128]{1,0:T(8,128)(2,1)S(1)} %get-tuple-element.29), channel_id=1, source_target_pairs={{0,48},{16,0},{32,16},{48,32},{1,17},{17,33},{33,49},{49,1},{2,50}... | collective-permute-start | bytes 491528 | tf_op jit(solution)/shard_map/ppermute | solution.py:219
  25.7 7.1 %collective-permute-start.9 = (bf16[640,128]{1,0:T(8,128)(2,1)S(1)}, bf16[640,128]{1,0:T(8,128)(2,1)S(1)}, u32[]{:S(2)}, u32[]{:S(2)}) collective-permute-start(bf16[640,128]{1,0:T(8,128)(2,1)S(1)} %get-tuple-element.25.after), channel_id=1, source_target_pairs={{0,16},{16,32},{32,48},{48,0},{1,49},{17,1},{33,17},{49,33},{2,18}... | collective-permute-start | bytes 491528 | tf_op jit(solution)/shard_map/ppermute | solution.py:219
  27.7 13.0 %collective-permute-start.13 = (bf16[512,128]{1,0:T(8,128)(2,1)S(1)}, bf16[512,128]{1,0:T(8,128)(2,1)S(1)}, u32[]{:S(2)}, u32[]{:S(2)}) collective-permute-start(bf16[512,128]{1,0:T(8,128)(2,1)S(1)} %get-tuple-element.32), channel_id=1, source_target_pairs={{0,32},{16,48},{32,0},{48,16},{1,33},{17,49},{33,1},{49,17},{2,34}... | collective-permute-start | bytes 393224 | tf_op jit(solution)/shard_map/ppermute | solution.py:219
  28.0 12.7 %collective-permute-start.12 = (bf16[512,128]{1,0:T(8,128)(2,1)S(1)}, bf16[512,128]{1,0:T(8,128)(2,1)S(1)}, u32[]{:S(2)}, u32[]{:S(2)}) collective-permute-start(bf16[512,128]{1,0:T(8,128)(2,1)S(1)} %get-tuple-element.31), channel_id=1, source_target_pairs={{0,16},{16,32},{32,48},{48,0},{1,49},{17,1},{33,17},{49,33},{2,18}... | collective-permute-start | bytes 393224 | tf_op jit(solution)/shard_map/ppermute | solution.py:219
  30.1 10.6 %collective-permute-start.14 = (bf16[512,128]{1,0:T(8,128)(2,1)S(1)}, bf16[512,128]{1,0:T(8,128)(2,1)S(1)}, u32[]{:S(2)}, u32[]{:S(2)}) collective-permute-start(bf16[512,128]{1,0:T(8,128)(2,1)S(1)} %get-tuple-element.33), channel_id=1, source_target_pairs={{0,48},{16,0},{32,16},{48,32},{1,17},{17,33},{33,49},{49,1},{2,50}... | collective-permute-start | bytes 393224 | tf_op jit(solution)/shard_map/ppermute | solution.py:219
  32.9 11.6 %collective-permute-start.16 = (bf16[384,128]{1,0:T(8,128)(2,1)S(1)}, bf16[384,128]{1,0:T(8,128)(2,1)S(1)}, u32[]{:S(2)}, u32[]{:S(2)}) collective-permute-start(bf16[384,128]{1,0:T(8,128)(2,1)S(1)} %get-tuple-element.36), channel_id=1, source_target_pairs={{0,128},{64,192},{128,0},{192,64},{1,129},{65,193},{129,1},{193,65... | collective-permute-start | bytes 294920 | tf_op jit(solution)/shard_map/ppermute | solution.py:219
  39.5 8.4 %collective-permute-start.17 = (bf16[384,128]{1,0:T(8,128)(2,1)S(1)}, bf16[384,128]{1,0:T(8,128)(2,1)S(1)}, u32[]{:S(2)}, u32[]{:S(2)}) collective-permute-start(bf16[384,128]{1,0:T(8,128)(2,1)S(1)} %get-tuple-element.37), channel_id=1, source_target_pairs={{0,192},{64,0},{128,64},{192,128},{1,65},{65,129},{129,193},{193,1... | collective-permute-start | bytes 294920 | tf_op jit(solution)/shard_map/ppermute | solution.py:219
  40.8 10.4 %collective-permute-start.15 = (bf16[384,128]{1,0:T(8,128)(2,1)S(1)}, bf16[384,128]{1,0:T(8,128)(2,1)S(1)}, u32[]{:S(2)}, u32[]{:S(2)}) collective-permute-start(bf16[384,128]{1,0:T(8,128)(2,1)S(1)} %get-tuple-element.35), channel_id=1, source_target_pairs={{0,64},{64,128},{128,192},{192,0},{1,193},{65,1},{129,65},{193,129... | collective-permute-start | bytes 294920 | tf_op jit(solution)/shard_map/ppermute | solution.py:219

commit v2 on v1

--- a/solution.py
+++ b/solution.py
@@ -257,7 +257,7 @@
     swapped = []
     for k in range(4):
         ready = got[k]
-        if k == 3:
+        if k == 2:
             ready, _ = lax.optimization_barrier((ready, order))
         swapped.append(lax.ppermute(ready, "core", swap))
     cost = lambda share: pl.CostEstimate(

time: 51.9 us -> 53.8 us (1.037)
  starting transfers between devices: 31.9 us -> 33.1 us
  waiting for transfers between devices: 11.3 us -> 12.5 us
    ppermute x9, waiting for transfers between devices: 9.32 us -> 10.5 us  [around(): return lax.ppermute(value, (axis, 'core'), pairs)]
    ppermute x4, starting transfers between devices: 7.32 us -> 7.93 us  [body(): got = [lax.ppermute(mine, COLS, chip_perm(k)) for k in range(4)]]
    ppermute x9, starting transfers between devices: 18.5 us -> 19.1 us  [around(): return lax.ppermute(value, (axis, 'core'), pairs)]
  transfers between devices with their start and end apart: 18 -> 18, of which waited for: 8 -> 7; matrix products, arithmetic and copies ran while one was open for 0% -> 0% of each run, Pallas kernels for 7% -> 6%
where the time goes in v2:
time: 53.8 us; the launch traced here: 54.1 us
  starting transfers between devices  33.1 us (62%)
  waiting for transfers between devices  12.5 us (23%)
  Pallas kernels  6.14 us (11%)
  between operations  1.4 us (3%)
  other arithmetic  0.94 us (2%)
    ppermute x9, starting transfers between devices, around(): return lax.ppermute(value, (axis, 'core'), pairs)  19.1 us
    ppermute x9, waiting for transfers between devices, around(): return lax.ppermute(value, (axis, 'core'), pairs)  10.5 us
    ppermute x4, starting transfers between devices, body(): got = [lax.ppermute(mine, COLS, chip_perm(k)) for k in range(4)]  7.93 us
    ppermute x1, starting transfers between devices, body(): lax.ppermute(local, 'core', swap)  3.33 us
    ppermute x4, starting transfers between devices, body(): swapped.append(lax.ppermute(ready, 'core', swap))  2.66 us
    pallas_call x1, Pallas kernels, body(): call(order_kernel, [pltpu.SMEM((1, PLACES), i32), pltpu.VMEM((SLOTS, T, T...  1.97 us
    pallas_call x1, Pallas kernels, body(): call(first_kernel, [struct(BLOCKS, T, T), struct(T, T), early, late], [sm...  1.33 us
    ppermute x4, waiting for transfers between devices, body(): swapped.append(lax.ppermute(ready, 'core', swap))  1.12 us
  transfers between devices with their start and end apart: 18, of which 7 were waited for; matrix products, arithmetic and copies ran while one was open for 0% of the time, Pallas kernels for 6%

profile of v2, /device:TPU:1, one launch (start us, length us, event | category | flops | bytes accessed | tf_op | source)
XLA Modules:
  0.0 54.1 jit_solution(1618430537711124337)
XLA Ops:
  0.6 0.9 %pad_maximum_fusion.inputs = bf16[896,128]{1,0:T(8,128)(2,1)S(1)} fusion(bf16[128,128]{1,0:T(8,128)(2,1)} %param.10, bf16[256,128]{1,0:T(8,128)(2,1)} %param.9, bf16[256,128]{1,0:T(8,128)(2,1)} %param.8, bf16[256,128]{1,0:T(8,128)(2,1)} %param.7), kind=kLoop, calls=%fused_computation | loop fusion | flops 917504 | bytes 458752 | tf_op jit(solution)/shard_map/concatenate | solution.py:237
  1.6 0.2 shard_map.87.own
  1.8 3.3 %collective-permute-start = (bf16[256,256]{1,0:T(8,128)(2,1)S(1)}, bf16[256,256]{1,0:T(8,128)(2,1)S(1)}, u32[]{:S(2)}, u32[]{:S(2)}) collective-permute-start(bf16[256,256]{1,0:T(8,128)(2,1)S(1)} %shard_map.87.own), channel_id=1, source_target_pairs={{0,1},{1,0},{2,3},{3,2},{4,5},{5,4},{6,7},{7,6},{8,9},{9,8},{10,11... | collective-permute-start | bytes 393224 | tf_op jit(solution)/shard_map/ppermute | solution.py:241
  5.1 0.1 stack.23.pos
  5.2 0.9 %collective-permute-done.other = bf16[256,256]{1,0:T(8,128)(2,1)S(1)} collective-permute-done((bf16[256,256]{1,0:T(8,128)(2,1)S(1)}, bf16[256,256]{1,0:T(8,128)(2,1)S(1)}, u32[]{:S(2)}, u32[]{:S(2)}) %collective-permute-start) | collective-permute-done | bytes 131104 | tf_op jit(solution)/shard_map/ppermute | solution.py:241
  6.1 0.6 %shard_map.88.refs_0_ = bf16[320,256]{1,0:T(8,128)(2,1)S(1)} custom-call(s32[5]{0:T(128)S(1)} %stack.23.pos, bf16[256,256]{1,0:T(8,128)(2,1)S(1)} %shard_map.87.own, bf16[256,256]{1,0:T(8,128)(2,1)S(1)} %collective-permute-done.other), custom_call_target="tpu_custom_call" | custom-call | tf_op jit(solution)/shard_map/pallas_call | solution.py:240
  6.7 2.4 %collective-permute-start.3 = (bf16[320,256]{1,0:T(8,128)(2,1)S(1)}, bf16[320,256]{1,0:T(8,128)(2,1)S(1)}, u32[]{:S(2)}, u32[]{:S(2)}) collective-permute-start(bf16[320,256]{1,0:T(8,128)(2,1)S(1)} %shard_map.88.refs_0_), channel_id=1, source_target_pairs={{0,4},{1,13},{2,6},{3,15},{4,0},{5,9},{6,2},{7,11},{8,12},{9,5},{1... | collective-permute-start | bytes 491528 | tf_op jit(solution)/shard_map/ppermute | solution.py:256
  9.1 3.6 %collective-permute-start.2 = (bf16[320,256]{1,0:T(8,128)(2,1)S(1)}, bf16[320,256]{1,0:T(8,128)(2,1)S(1)}, u32[]{:S(2)}, u32[]{:S(2)}) collective-permute-start(bf16[320,256]{1,0:T(8,128)(2,1)S(1)} %shard_map.88.refs_0_), channel_id=1, source_target_pairs={{0,2},{1,15},{2,4},{3,9},{4,6},{5,11},{6,0},{7,13},{8,10},{9,7},{1... | collective-permute-start | bytes 491528 | tf_op jit(solution)/shard_map/ppermute | solution.py:256
  12.7 1.9 %collective-permute-start.1 = (bf16[320,256]{1,0:T(8,128)(2,1)S(1)}, bf16[320,256]{1,0:T(8,128)(2,1)S(1)}, u32[]{:S(2)}, u32[]{:S(2)}) collective-permute-start(bf16[320,256]{1,0:T(8,128)(2,1)S(1)} %shard_map.88.refs_0_), channel_id=1, source_target_pairs={{1,9},{3,11},{5,13},{7,15},{9,1},{11,3},{13,5},{15,7},{17,25},{19,... | collective-permute-start | bytes 491528 | tf_op jit(solution)/shard_map/ppermute | solution.py:256
  15.3 2.0 %shard_map.86 = (s32[1,1024]{1,0:T(1,128)S(4)}, bf16[256,128,128]{2,1,0:T(8,128)(2,1)S(1)}) custom-call(s32[5]{0:T(128)S(1)} %stack.23.pos, s32[1]{0:T(128)} %bitcast.8.count_ref, s32[2,256]{1,0:T(2,128)} %bitcast.10, bf16[256,128,128]{2,1,0:T(8,128)(2,1)} %bitcast.9), custom_call_target="tpu_custom_call" | custom-call | bytes 16777216 | tf_op jit(solution)/shard_map/pallas_call | solution.py:243
  17.3 0.5 collective-permute-start.8
  17.8 1.6 %collective-permute-start.6 = (bf16[320,256]{1,0:T(8,128)(2,1)S(1)}, bf16[320,256]{1,0:T(8,128)(2,1)S(1)}, u32[]{:S(2)}, u32[]{:S(2)}) collective-permute-start(bf16[320,256]{1,0:T(8,128)(2,1)S(1)} %collective-permute-done.2.refs_2_), channel_id=1, source_target_pairs={{0,1},{1,0},{2,3},{3,2},{4,5},{5,4},{6,7},{7,6},{8,9},{9,8},{10,11... | collective-permute-start | bytes 491528 | tf_op jit(solution)/shard_map/ppermute | solution.py:262
  19.4 0.5 collective-permute-start.7
  19.9 0.5 collective-permute-done.6.refs_6_
  20.4 0.4 collective-permute-done.5.refs_5_
  20.8 0.2 collective-permute-done.7.refs_7_
  21.0 1.3 %shard_map.89 = (bf16[32,128,128]{2,1,0:T(8,128)(2,1)S(1)}, bf16[128,128]{1,0:T(8,128)(2,1)S(1)}, bf16[640,128]{1,0:T(8,128)(2,1)S(1)}, bf16[512,128]{1,0:T(8,128)(2,1)S(1)}) custom-call(s32[5]{0:T(128)S(1)} %stack.23.pos, s32[1,1024]{1,0:T(1,128)S(4)} %get-tuple-element.20.order, bf16[320,256]{1,0:T(8,128)(2,1)S(1)} %shard_map.88.refs_0_, ...), custom_call_target="tpu_custom_call" | custom-call | flops 1073741824 | bytes 8388608 | tf_op jit(solution)/shard_map/pallas_call | solution.py:267
  22.4 2.3 %collective-permute-start.10 = (bf16[640,128]{1,0:T(8,128)(2,1)S(1)}, bf16[640,128]{1,0:T(8,128)(2,1)S(1)}, u32[]{:S(2)}, u32[]{:S(2)}) collective-permute-start(bf16[640,128]{1,0:T(8,128)(2,1)S(1)} %get-tuple-element.28), channel_id=1, source_target_pairs={{0,32},{16,48},{32,0},{48,16},{1,33},{17,49},{33,1},{49,17},{2,34}... | collective-permute-start | bytes 491528 | tf_op jit(solution)/shard_map/ppermute | solution.py:219
  24.7 0.6 %shard_map.90 = (bf16[640,128]{1,0:T(8,128)(2,1)S(1)}, bf16[512,128]{1,0:T(8,128)(2,1)S(1)}, bf16[640,128]{1,0:T(8,128)(2,1)S(1)}, bf16[512,128]{1,0:T(8,128)(2,1)S(1)}) custom-call(s32[1,1024]{1,0:T(1,128)S(4)} %get-tuple-element.20.order, bf16[32,128,128]{2,1,0:T(8,128)(2,1)S(1)} %get-tuple-element.23.grads, ...), custom_call_target="tpu_custom_call" | custom-call | flops 1073741824 | bytes 8388608 | tf_op jit(solution)/shard_map/pallas_call | solution.py:274
  25.3 2.7 %collective-permute-start.11 = (bf16[640,128]{1,0:T(8,128)(2,1)S(1)}, bf16[640,128]{1,0:T(8,128)(2,1)S(1)}, u32[]{:S(2)}, u32[]{:S(2)}) collective-permute-start(bf16[640,128]{1,0:T(8,128)(2,1)S(1)} %get-tuple-element.29), channel_id=1, source_target_pairs={{0,48},{16,0},{32,16},{48,32},{1,17},{17,33},{33,49},{49,1},{2,50}... | collective-permute-start | bytes 491528 | tf_op jit(solution)/shard_map/ppermute | solution.py:219
  28.0 1.0 %collective-permute-start.9 = (bf16[640,128]{1,0:T(8,128)(2,1)S(1)}, bf16[640,128]{1,0:T(8,128)(2,1)S(1)}, u32[]{:S(2)}, u32[]{:S(2)}) collective-permute-start(bf16[640,128]{1,0:T(8,128)(2,1)S(1)} %get-tuple-element.25.after), channel_id=1, source_target_pairs={{0,16},{16,32},{32,48},{48,0},{1,49},{17,1},{33,17},{49,33},{2,18}... | collective-permute-start | bytes 491528 | tf_op jit(solution)/shard_map/ppermute | solution.py:219
  29.0 1.1 %collective-permute-start.13 = (bf16[512,128]{1,0:T(8,128)(2,1)S(1)}, bf16[512,128]{1,0:T(8,128)(2,1)S(1)}, u32[]{:S(2)}, u32[]{:S(2)}) collective-permute-start(bf16[512,128]{1,0:T(8,128)(2,1)S(1)} %get-tuple-element.32), channel_id=1, source_target_pairs={{0,32},{16,48},{32,0},{48,16},{1,33},{17,49},{33,1},{49,17},{2,34}... | collective-permute-start | bytes 393224 | tf_op jit(solution)/shard_map/ppermute | solution.py:219
  30.1 1.8 %collective-permute-start.12 = (bf16[512,128]{1,0:T(8,128)(2,1)S(1)}, bf16[512,128]{1,0:T(8,128)(2,1)S(1)}, u32[]{:S(2)}, u32[]{:S(2)}) collective-permute-start(bf16[512,128]{1,0:T(8,128)(2,1)S(1)} %get-tuple-element.31), channel_id=1, source_target_pairs={{0,16},{16,32},{32,48},{48,0},{1,49},{17,1},{33,17},{49,33},{2,18}... | collective-permute-start | bytes 393224 | tf_op jit(solution)/shard_map/ppermute | solution.py:219
  31.9 0.6 %shard_map.91 = (f32[512,128]{1,0:T(8,128)S(1)}, f32[512,128]{1,0:T(8,128)S(1)}) custom-call(s32[1,1024]{1,0:T(1,128)S(4)} %get-tuple-element.20.order, bf16[32,128,128]{2,1,0:T(8,128)(2,1)S(1)} %get-tuple-element.23.grads, bf16[256,128,128]{2,1,0:T(8,128)(2,1)S(1)} %get-tuple-element.22.refs_9_.tiles, bf16[640,128]{1,0:T(8,128)(2,1)S(1)} %get-tuple-element.25.after), custom_call_target="tpu_custom_call" | custom-call | flops 1073741824 | bytes 8388608 | tf_op jit(solution)/shard_map/pallas_call | solution.py:281
  32.5 2.8 %collective-permute-done.9.r1 = bf16[640,128]{1,0:T(8,128)(2,1)S(1)} collective-permute-done((bf16[640,128]{1,0:T(8,128)(2,1)S(1)}, bf16[640,128]{1,0:T(8,128)(2,1)S(1)}, u32[]{:S(2)}, u32[]{:S(2)}) %collective-permute-start.9) | collective-permute-done | bytes 163872 | tf_op jit(solution)/shard_map/ppermute | solution.py:219
  35.3 0.1 shard_map.92
  35.4 4.3 %collective-permute-start.16 = (bf16[384,128]{1,0:T(8,128)(2,1)S(1)}, bf16[384,128]{1,0:T(8,128)(2,1)S(1)}, u32[]{:S(2)}, u32[]{:S(2)}) collective-permute-start(bf16[384,128]{1,0:T(8,128)(2,1)S(1)} %get-tuple-element.36), channel_id=1, source_target_pairs={{0,128},{64,192},{128,0},{192,64},{1,129},{65,193},{129,1},{193,65... | collective-permute-start | bytes 294920 | tf_op jit(solution)/shard_map/ppermute | solution.py:219
  39.7 2.5 %collective-permute-start.17 = (bf16[384,128]{1,0:T(8,128)(2,1)S(1)}, bf16[384,128]{1,0:T(8,128)(2,1)S(1)}, u32[]{:S(2)}, u32[]{:S(2)}) collective-permute-start(bf16[384,128]{1,0:T(8,128)(2,1)S(1)} %get-tuple-element.37), channel_id=1, source_target_pairs={{0,192},{64,0},{128,64},{192,128},{1,65},{65,129},{129,193},{193,1... | collective-permute-start | bytes 294920 | tf_op jit(solution)/shard_map/ppermute | solution.py:219
  42.3 3.4 %collective-permute-start.15 = (bf16[384,128]{1,0:T(8,128)(2,1)S(1)}, bf16[384,128]{1,0:T(8,128)(2,1)S(1)}, u32[]{:S(2)}, u32[]{:S(2)}) collective-permute-start(bf16[384,128]{1,0:T(8,128)(2,1)S(1)} %get-tuple-element.35), channel_id=1, source_target_pairs={{0,64},{64,128},{128,192},{192,0},{1,193},{65,1},{129,65},{193,129... | collective-permute-start | bytes 294920 | tf_op jit(solution)/shard_map/ppermute | solution.py:219
  45.7 0.9 %collective-permute-done.17.r3 = bf16[384,128]{1,0:T(8,128)(2,1)S(1)} collective-permute-done((bf16[384,128]{1,0:T(8,128)(2,1)S(1)}, bf16[384,128]{1,0:T(8,128)(2,1)S(1)}, u32[]{:S(2)}, u32[]{:S(2)}) %collective-permute-start.17) | collective-permute-done | bytes 98336 | tf_op jit(solution)/shard_map/ppermute | solution.py:219
  46.6 6.7 %collective-permute-done.15.r1 = bf16[384,128]{1,0:T(8,128)(2,1)S(1)} collective-permute-done((bf16[384,128]{1,0:T(8,128)(2,1)S(1)}, bf16[384,128]{1,0:T(8,128)(2,1)S(1)}, u32[]{:S(2)}, u32[]{:S(2)}) %collective-permute-start.15) | collective-permute-done | bytes 98336 | tf_op jit(solution)/shard_map/ppermute | solution.py:219
  53.4 0.7 %shard_map.94 = (bf16[256,128]{1,0:T(8,128)(2,1)}, f32[128,128]{1,0:T(8,128)}) custom-call(f32[256,128]{1,0:T(8,128)S(1)} %get-tuple-element.34.keep, bf16[128,128]{1,0:T(8,128)(2,1)S(1)} %get-tuple-element.30.weight_y, bf16[384,128]{1,0:T(8,128)(2,1)S(1)} %collective-permute-done.15.r1, bf16[384,128]{1,0:T(8,128)(2,1)S(1)} %collective-permute-done.16.r2, ...), custom_call_target="tpu_custom_call" | custom-call | tf_op jit(solution)/shard_map/pallas_call | solution.py:302
  (15 shorter events, 0.2 us)
Async XLA Ops:
  1.8 4.3 %collective-permute-start = (bf16[256,256]{1,0:T(8,128)(2,1)S(1)}, bf16[256,256]{1,0:T(8,128)(2,1)S(1)}, u32[]{:S(2)}, u32[]{:S(2)}) collective-permute-start(bf16[256,256]{1,0:T(8,128)(2,1)S(1)} %shard_map.87.own), channel_id=1, source_target_pairs={{0,1},{1,0},{2,3},{3,2},{4,5},{5,4},{6,7},{7,6},{8,9},{9,8},{10,11... | collective-permute-start | bytes 393224 | tf_op jit(solution)/shard_map/ppermute | solution.py:241
  6.7 10.6 %collective-permute-start.3 = (bf16[320,256]{1,0:T(8,128)(2,1)S(1)}, bf16[320,256]{1,0:T(8,128)(2,1)S(1)}, u32[]{:S(2)}, u32[]{:S(2)}) collective-permute-start(bf16[320,256]{1,0:T(8,128)(2,1)S(1)} %shard_map.88.refs_0_), channel_id=1, source_target_pairs={{0,4},{1,13},{2,6},{3,15},{4,0},{5,9},{6,2},{7,11},{8,12},{9,5},{1... | collective-permute-start | bytes 491528 | tf_op jit(solution)/shard_map/ppermute | solution.py:256
  9.1 8.1 %collective-permute-start.4 = (bf16[320,256]{1,0:T(8,128)(2,1)S(1)}, bf16[320,256]{1,0:T(8,128)(2,1)S(1)}, u32[]{:S(2)}, u32[]{:S(2)}) collective-permute-start(bf16[320,256]{1,0:T(8,128)(2,1)S(1)} %shard_map.88.refs_0_), channel_id=1, source_target_pairs={{0,6},{1,11},{2,0},{3,13},{4,2},{5,15},{6,4},{7,9},{8,14},{9,3},{1... | collective-permute-start | bytes 491528 | tf_op jit(solution)/shard_map/ppermute | solution.py:256
  9.1 8.7 %collective-permute-start.2 = (bf16[320,256]{1,0:T(8,128)(2,1)S(1)}, bf16[320,256]{1,0:T(8,128)(2,1)S(1)}, u32[]{:S(2)}, u32[]{:S(2)}) collective-permute-start(bf16[320,256]{1,0:T(8,128)(2,1)S(1)} %shard_map.88.refs_0_), channel_id=1, source_target_pairs={{0,2},{1,15},{2,4},{3,9},{4,6},{5,11},{6,0},{7,13},{8,10},{9,7},{1... | collective-permute-start | bytes 491528 | tf_op jit(solution)/shard_map/ppermute | solution.py:256
  12.7 6.7 %collective-permute-start.1 = (bf16[320,256]{1,0:T(8,128)(2,1)S(1)}, bf16[320,256]{1,0:T(8,128)(2,1)S(1)}, u32[]{:S(2)}, u32[]{:S(2)}) collective-permute-start(bf16[320,256]{1,0:T(8,128)(2,1)S(1)} %shard_map.88.refs_0_), channel_id=1, source_target_pairs={{1,9},{3,11},{5,13},{7,15},{9,1},{11,3},{13,5},{15,7},{17,25},{19,... | collective-permute-start | bytes 491528 | tf_op jit(solution)/shard_map/ppermute | solution.py:256
  17.3 2.7 %collective-permute-start.8 = (bf16[320,256]{1,0:T(8,128)(2,1)S(1)}, bf16[320,256]{1,0:T(8,128)(2,1)S(1)}, u32[]{:S(2)}, u32[]{:S(2)}) collective-permute-start(bf16[320,256]{1,0:T(8,128)(2,1)S(1)} %collective-permute-done.4.refs_4_), channel_id=1, source_target_pairs={{0,1},{1,0},{2,3},{3,2},{4,5},{5,4},{6,7},{7,6},{8,9},{9,8},{10,11... | collective-permute-start | bytes 491528 | tf_op jit(solution)/shard_map/ppermute | solution.py:262
  17.8 2.7 %collective-permute-start.6 = (bf16[320,256]{1,0:T(8,128)(2,1)S(1)}, bf16[320,256]{1,0:T(8,128)(2,1)S(1)}, u32[]{:S(2)}, u32[]{:S(2)}) collective-permute-start(bf16[320,256]{1,0:T(8,128)(2,1)S(1)} %collective-permute-done.2.refs_2_), channel_id=1, source_target_pairs={{0,1},{1,0},{2,3},{3,2},{4,5},{5,4},{6,7},{7,6},{8,9},{9,8},{10,11... | collective-permute-start | bytes 491528 | tf_op jit(solution)/shard_map/ppermute | solution.py:262
  19.4 1.4 %collective-permute-start.5 = (bf16[320,256]{1,0:T(8,128)(2,1)S(1)}, bf16[320,256]{1,0:T(8,128)(2,1)S(1)}, u32[]{:S(2)}, u32[]{:S(2)}) collective-permute-start(bf16[320,256]{1,0:T(8,128)(2,1)S(1)} %collective-permute-done.1.refs_1_), channel_id=1, source_target_pairs={{0,1},{1,0},{2,3},{3,2},{4,5},{5,4},{6,7},{7,6},{8,9},{9,8},{10,11... | collective-permute-start | bytes 491528 | tf_op jit(solution)/shard_map/ppermute | solution.py:262
  19.4 1.6 %collective-permute-start.7 = (bf16[320,256]{1,0:T(8,128)(2,1)S(1)}, bf16[320,256]{1,0:T(8,128)(2,1)S(1)}, u32[]{:S(2)}, u32[]{:S(2)}) collective-permute-start(bf16[320,256]{1,0:T(8,128)(2,1)S(1)} %collective-permute-done.3.refs_3_), channel_id=1, source_target_pairs={{0,1},{1,0},{2,3},{3,2},{4,5},{5,4},{6,7},{7,6},{8,9},{9,8},{10,11... | collective-permute-start | bytes 491528 | tf_op jit(solution)/shard_map/ppermute | solution.py:262
  22.4 10.0 %collective-permute-start.10 = (bf16[640,128]{1,0:T(8,128)(2,1)S(1)}, bf16[640,128]{1,0:T(8,128)(2,1)S(1)}, u32[]{:S(2)}, u32[]{:S(2)}) collective-permute-start(bf16[640,128]{1,0:T(8,128)(2,1)S(1)} %get-tuple-element.28), channel_id=1, source_target_pairs={{0,32},{16,48},{32,0},{48,16},{1,33},{17,49},{33,1},{49,17},{2,34}... | collective-permute-start | bytes 491528 | tf_op jit(solution)/shard_map/ppermute | solution.py:219
  25.3 7.2 %collective-permute-start.11 = (bf16[640,128]{1,0:T(8,128)(2,1)S(1)}, bf16[640,128]{1,0:T(8,128)(2,1)S(1)}, u32[]{:S(2)}, u32[]{:S(2)}) collective-permute-start(bf16[640,128]{1,0:T(8,128)(2,1)S(1)} %get-tuple-element.29), channel_id=1, source_target_pairs={{0,48},{16,0},{32,16},{48,32},{1,17},{17,33},{33,49},{49,1},{2,50}... | collective-permute-start | bytes 491528 | tf_op jit(solution)/shard_map/ppermute | solution.py:219
  28.0 7.3 %collective-permute-start.9 = (bf16[640,128]{1,0:T(8,128)(2,1)S(1)}, bf16[640,128]{1,0:T(8,128)(2,1)S(1)}, u32[]{:S(2)}, u32[]{:S(2)}) collective-permute-start(bf16[640,128]{1,0:T(8,128)(2,1)S(1)} %get-tuple-element.25.after), channel_id=1, source_target_pairs={{0,16},{16,32},{32,48},{48,0},{1,49},{17,1},{33,17},{49,33},{2,18}... | collective-permute-start | bytes 491528 | tf_op jit(solution)/shard_map/ppermute | solution.py:219
  29.0 13.2 %collective-permute-start.13 = (bf16[512,128]{1,0:T(8,128)(2,1)S(1)}, bf16[512,128]{1,0:T(8,128)(2,1)S(1)}, u32[]{:S(2)}, u32[]{:S(2)}) collective-permute-start(bf16[512,128]{1,0:T(8,128)(2,1)S(1)} %get-tuple-element.32), channel_id=1, source_target_pairs={{0,32},{16,48},{32,0},{48,16},{1,33},{17,49},{33,1},{49,17},{2,34}... | collective-permute-start | bytes 393224 | tf_op jit(solution)/shard_map/ppermute | solution.py:219
  30.1 12.1 %collective-permute-start.12 = (bf16[512,128]{1,0:T(8,128)(2,1)S(1)}, bf16[512,128]{1,0:T(8,128)(2,1)S(1)}, u32[]{:S(2)}, u32[]{:S(2)}) collective-permute-start(bf16[512,128]{1,0:T(8,128)(2,1)S(1)} %get-tuple-element.31), channel_id=1, source_target_pairs={{0,16},{16,32},{32,48},{48,0},{1,49},{17,1},{33,17},{49,33},{2,18}... | collective-permute-start | bytes 393224 | tf_op jit(solution)/shard_map/ppermute | solution.py:219
  32.4 9.8 %collective-permute-start.14 = (bf16[512,128]{1,0:T(8,128)(2,1)S(1)}, bf16[512,128]{1,0:T(8,128)(2,1)S(1)}, u32[]{:S(2)}, u32[]{:S(2)}) collective-permute-start(bf16[512,128]{1,0:T(8,128)(2,1)S(1)} %get-tuple-element.33), channel_id=1, source_target_pairs={{0,48},{16,0},{32,16},{48,32},{1,17},{17,33},{33,49},{49,1},{2,50}... | collective-permute-start | bytes 393224 | tf_op jit(solution)/shard_map/ppermute | solution.py:219
  35.4 10.3 %collective-permute-start.16 = (bf16[384,128]{1,0:T(8,128)(2,1)S(1)}, bf16[384,128]{1,0:T(8,128)(2,1)S(1)}, u32[]{:S(2)}, u32[]{:S(2)}) collective-permute-start(bf16[384,128]{1,0:T(8,128)(2,1)S(1)} %get-tuple-element.36), channel_id=1, source_target_pairs={{0,128},{64,192},{128,0},{192,64},{1,129},{65,193},{129,1},{193,65... | collective-permute-start | bytes 294920 | tf_op jit(solution)/shard_map/ppermute | solution.py:219
  39.7 6.9 %collective-permute-start.17 = (bf16[384,128]{1,0:T(8,128)(2,1)S(1)}, bf16[384,128]{1,0:T(8,128)(2,1)S(1)}, u32[]{:S(2)}, u32[]{:S(2)}) collective-permute-start(bf16[384,128]{1,0:T(8,128)(2,1)S(1)} %get-tuple-element.37), channel_id=1, source_target_pairs={{0,192},{64,0},{128,64},{192,128},{1,65},{65,129},{129,193},{193,1... | collective-permute-start | bytes 294920 | tf_op jit(solution)/shard_map/ppermute | solution.py:219
  42.3 11.1 %collective-permute-start.15 = (bf16[384,128]{1,0:T(8,128)(2,1)S(1)}, bf16[384,128]{1,0:T(8,128)(2,1)S(1)}, u32[]{:S(2)}, u32[]{:S(2)}) collective-permute-start(bf16[384,128]{1,0:T(8,128)(2,1)S(1)} %get-tuple-element.35), channel_id=1, source_target_pairs={{0,64},{64,128},{128,192},{192,0},{1,193},{65,1},{129,65},{193,129... | collective-permute-start | bytes 294920 | tf_op jit(solution)/shard_map/ppermute | solution.py:219

commit v3 on v2

--- a/solution.py
+++ b/solution.py
@@ -257,7 +257,7 @@
     swapped = []
     for k in range(4):
         ready = got[k]
-        if k == 2:
+        if k == 0:
             ready, _ = lax.optimization_barrier((ready, order))
         swapped.append(lax.ppermute(ready, "core", swap))
     cost = lambda share: pl.CostEstimate(

time: 53.8 us -> 53.9 us (level); the launches traced: 54.1 us -> 52.9 us
  waiting for transfers between devices: 12.5 us -> 10.2 us
  starting transfers between devices: 33.1 us -> 34.2 us
    ppermute x9, waiting for transfers between devices: 10.5 us -> 6.84 us  [around(): return lax.ppermute(value, (axis, 'core'), pairs)]
    ppermute x9, starting transfers between devices: 19.1 us -> 20.3 us  [around(): return lax.ppermute(value, (axis, 'core'), pairs)]
    ppermute x4, waiting for transfers between devices: 0.01 us -> 1.03 us  [body(): got = [lax.ppermute(mine, COLS, chip_perm(k)) for k in range(4)]]
    ppermute x4, starting transfers between devices: 7.93 us -> 7.33 us  [body(): got = [lax.ppermute(mine, COLS, chip_perm(k)) for k in range(4)]]
    ppermute x4, starting transfers between devices: 2.66 us -> 3.21 us  [body(): swapped.append(lax.ppermute(ready, 'core', swap))]
where the time goes in v3:
time: 53.9 us; the launch traced here: 52.9 us
  starting transfers between devices  34.2 us (63%)
  waiting for transfers between devices  10.2 us (19%)
  Pallas kernels  6.12 us (11%)
  between operations  1.42 us (3%)
  other arithmetic  0.94 us (2%)
    ppermute x9, starting transfers between devices, around(): return lax.ppermute(value, (axis, 'core'), pairs)  20.3 us
    ppermute x4, starting transfers between devices, body(): got = [lax.ppermute(mine, COLS, chip_perm(k)) for k in range(4)]  7.33 us
    ppermute x9, waiting for transfers between devices, around(): return lax.ppermute(value, (axis, 'core'), pairs)  6.84 us
    ppermute x1, starting transfers between devices, body(): lax.ppermute(local, 'core', swap)  3.33 us
    ppermute x4, starting transfers between devices, body(): swapped.append(lax.ppermute(ready, 'core', swap))  3.21 us
    pallas_call x1, Pallas kernels, body(): call(order_kernel, [pltpu.SMEM((1, PLACES), i32), pltpu.VMEM((SLOTS, T, T...  1.97 us
    ppermute x4, waiting for transfers between devices, body(): swapped.append(lax.ppermute(ready, 'core', swap))  1.39 us
    pallas_call x1, Pallas kernels, body(): call(first_kernel, [struct(BLOCKS, T, T), struct(T, T), early, late], [sm...  1.34 us
  transfers between devices with their start and end apart: 18, of which 7 were waited for; matrix products, arithmetic and copies ran while one was open for 0% of the time, Pallas kernels for 6%

profile of v3, /device:TPU:1, one launch (start us, length us, event | category | flops | bytes accessed | tf_op | source)
XLA Modules:
  0.0 52.9 jit_solution(425268294652343025)
XLA Ops:
  0.6 0.9 %pad_maximum_fusion.inputs = bf16[896,128]{1,0:T(8,128)(2,1)S(1)} fusion(bf16[128,128]{1,0:T(8,128)(2,1)} %param.10, bf16[256,128]{1,0:T(8,128)(2,1)} %param.9, bf16[256,128]{1,0:T(8,128)(2,1)} %param.8, bf16[256,128]{1,0:T(8,128)(2,1)} %param.7), kind=kLoop, calls=%fused_computation | loop fusion | flops 917504 | bytes 458752 | tf_op jit(solution)/shard_map/concatenate | solution.py:237
  1.6 0.2 shard_map.87.own
  1.8 3.3 %collective-permute-start = (bf16[256,256]{1,0:T(8,128)(2,1)S(1)}, bf16[256,256]{1,0:T(8,128)(2,1)S(1)}, u32[]{:S(2)}, u32[]{:S(2)}) collective-permute-start(bf16[256,256]{1,0:T(8,128)(2,1)S(1)} %shard_map.87.own), channel_id=1, source_target_pairs={{0,1},{1,0},{2,3},{3,2},{4,5},{5,4},{6,7},{7,6},{8,9},{9,8},{10,11... | collective-permute-start | bytes 393224 | tf_op jit(solution)/shard_map/ppermute | solution.py:241
  5.1 0.1 stack.23.pos
  5.2 0.9 %collective-permute-done.other = bf16[256,256]{1,0:T(8,128)(2,1)S(1)} collective-permute-done((bf16[256,256]{1,0:T(8,128)(2,1)S(1)}, bf16[256,256]{1,0:T(8,128)(2,1)S(1)}, u32[]{:S(2)}, u32[]{:S(2)}) %collective-permute-start) | collective-permute-done | bytes 131104 | tf_op jit(solution)/shard_map/ppermute | solution.py:241
  6.1 0.6 %shard_map.88.refs_0_ = bf16[320,256]{1,0:T(8,128)(2,1)S(1)} custom-call(s32[5]{0:T(128)S(1)} %stack.23.pos, bf16[256,256]{1,0:T(8,128)(2,1)S(1)} %shard_map.87.own, bf16[256,256]{1,0:T(8,128)(2,1)S(1)} %collective-permute-done.other), custom_call_target="tpu_custom_call" | custom-call | tf_op jit(solution)/shard_map/pallas_call | solution.py:240
  6.7 1.9 %collective-permute-start.1 = (bf16[320,256]{1,0:T(8,128)(2,1)S(1)}, bf16[320,256]{1,0:T(8,128)(2,1)S(1)}, u32[]{:S(2)}, u32[]{:S(2)}) collective-permute-start(bf16[320,256]{1,0:T(8,128)(2,1)S(1)} %shard_map.88.refs_0_), channel_id=1, source_target_pairs={{1,9},{3,11},{5,13},{7,15},{9,1},{11,3},{13,5},{15,7},{17,25},{19,... | collective-permute-start | bytes 491528 | tf_op jit(solution)/shard_map/ppermute | solution.py:256
  8.6 0.9 %collective-permute-start.4 = (bf16[320,256]{1,0:T(8,128)(2,1)S(1)}, bf16[320,256]{1,0:T(8,128)(2,1)S(1)}, u32[]{:S(2)}, u32[]{:S(2)}) collective-permute-start(bf16[320,256]{1,0:T(8,128)(2,1)S(1)} %shard_map.88.refs_0_), channel_id=1, source_target_pairs={{0,6},{1,11},{2,0},{3,13},{4,2},{5,15},{6,4},{7,9},{8,14},{9,3},{1... | collective-permute-start | bytes 491528 | tf_op jit(solution)/shard_map/ppermute | solution.py:256
  9.5 3.6 %collective-permute-start.3 = (bf16[320,256]{1,0:T(8,128)(2,1)S(1)}, bf16[320,256]{1,0:T(8,128)(2,1)S(1)}, u32[]{:S(2)}, u32[]{:S(2)}) collective-permute-start(bf16[320,256]{1,0:T(8,128)(2,1)S(1)} %shard_map.88.refs_0_), channel_id=1, source_target_pairs={{0,4},{1,13},{2,6},{3,15},{4,0},{5,9},{6,2},{7,11},{8,12},{9,5},{1... | collective-permute-start | bytes 491528 | tf_op jit(solution)/shard_map/ppermute | solution.py:256
  13.1 0.9 %collective-permute-start.2 = (bf16[320,256]{1,0:T(8,128)(2,1)S(1)}, bf16[320,256]{1,0:T(8,128)(2,1)S(1)}, u32[]{:S(2)}, u32[]{:S(2)}) collective-permute-start(bf16[320,256]{1,0:T(8,128)(2,1)S(1)} %shard_map.88.refs_0_), channel_id=1, source_target_pairs={{0,2},{1,15},{2,4},{3,9},{4,6},{5,11},{6,0},{7,13},{8,10},{9,7},{1... | collective-permute-start | bytes 491528 | tf_op jit(solution)/shard_map/ppermute | solution.py:256
  14.7 2.0 %shard_map.86 = (s32[1,1024]{1,0:T(1,128)S(4)}, bf16[256,128,128]{2,1,0:T(8,128)(2,1)S(1)}) custom-call(s32[5]{0:T(128)S(1)} %stack.23.pos, s32[1]{0:T(128)} %bitcast.8.count_ref, s32[2,256]{1,0:T(2,128)} %bitcast.10, bf16[256,128,128]{2,1,0:T(8,128)(2,1)} %bitcast.9), custom_call_target="tpu_custom_call" | custom-call | bytes 16777216 | tf_op jit(solution)/shard_map/pallas_call | solution.py:243
  16.7 0.1 collective-permute-start.8
  16.8 1.0 %collective-permute-done.3.refs_3_ = bf16[320,256]{1,0:T(8,128)(2,1)S(1)} collective-permute-done((bf16[320,256]{1,0:T(8,128)(2,1)S(1)}, bf16[320,256]{1,0:T(8,128)(2,1)S(1)}, u32[]{:S(2)}, u32[]{:S(2)}) %collective-permute-start.3) | collective-permute-done | bytes 163872 | tf_op jit(solution)/shard_map/ppermute | solution.py:256
  17.8 1.5 %collective-permute-start.7 = (bf16[320,256]{1,0:T(8,128)(2,1)S(1)}, bf16[320,256]{1,0:T(8,128)(2,1)S(1)}, u32[]{:S(2)}, u32[]{:S(2)}) collective-permute-start(bf16[320,256]{1,0:T(8,128)(2,1)S(1)} %collective-permute-done.3.refs_3_), channel_id=1, source_target_pairs={{0,1},{1,0},{2,3},{3,2},{4,5},{5,4},{6,7},{7,6},{8,9},{9,8},{10,11... | collective-permute-start | bytes 491528 | tf_op jit(solution)/shard_map/ppermute | solution.py:262
  19.3 1.6 %collective-permute-start.6 = (bf16[320,256]{1,0:T(8,128)(2,1)S(1)}, bf16[320,256]{1,0:T(8,128)(2,1)S(1)}, u32[]{:S(2)}, u32[]{:S(2)}) collective-permute-start(bf16[320,256]{1,0:T(8,128)(2,1)S(1)} %collective-permute-done.2.refs_2_), channel_id=1, source_target_pairs={{0,1},{1,0},{2,3},{3,2},{4,5},{5,4},{6,7},{7,6},{8,9},{9,8},{10,11... | collective-permute-start | bytes 491528 | tf_op jit(solution)/shard_map/ppermute | solution.py:262
  20.9 1.0 %collective-permute-done.6.refs_6_ = bf16[320,256]{1,0:T(8,128)(2,1)S(1)} collective-permute-done((bf16[320,256]{1,0:T(8,128)(2,1)S(1)}, bf16[320,256]{1,0:T(8,128)(2,1)S(1)}, u32[]{:S(2)}, u32[]{:S(2)}) %collective-permute-start.6) | collective-permute-done | bytes 163872 | tf_op jit(solution)/shard_map/ppermute | solution.py:262
  21.9 0.4 collective-permute-done.5.refs_5_
  22.3 1.3 %shard_map.89 = (bf16[32,128,128]{2,1,0:T(8,128)(2,1)S(1)}, bf16[128,128]{1,0:T(8,128)(2,1)S(1)}, bf16[640,128]{1,0:T(8,128)(2,1)S(1)}, bf16[512,128]{1,0:T(8,128)(2,1)S(1)}) custom-call(s32[5]{0:T(128)S(1)} %stack.23.pos, s32[1,1024]{1,0:T(1,128)S(4)} %get-tuple-element.20.order, bf16[320,256]{1,0:T(8,128)(2,1)S(1)} %shard_map.88.refs_0_, ...), custom_call_target="tpu_custom_call" | custom-call | flops 1073741824 | bytes 8388608 | tf_op jit(solution)/shard_map/pallas_call | solution.py:267
  23.6 3.0 %collective-permute-start.10 = (bf16[640,128]{1,0:T(8,128)(2,1)S(1)}, bf16[640,128]{1,0:T(8,128)(2,1)S(1)}, u32[]{:S(2)}, u32[]{:S(2)}) collective-permute-start(bf16[640,128]{1,0:T(8,128)(2,1)S(1)} %get-tuple-element.28), channel_id=1, source_target_pairs={{0,32},{16,48},{32,0},{48,16},{1,33},{17,49},{33,1},{49,17},{2,34}... | collective-permute-start | bytes 491528 | tf_op jit(solution)/shard_map/ppermute | solution.py:219
  26.6 0.6 %shard_map.90 = (bf16[640,128]{1,0:T(8,128)(2,1)S(1)}, bf16[512,128]{1,0:T(8,128)(2,1)S(1)}, bf16[640,128]{1,0:T(8,128)(2,1)S(1)}, bf16[512,128]{1,0:T(8,128)(2,1)S(1)}) custom-call(s32[1,1024]{1,0:T(1,128)S(4)} %get-tuple-element.20.order, bf16[32,128,128]{2,1,0:T(8,128)(2,1)S(1)} %get-tuple-element.23.grads, ...), custom_call_target="tpu_custom_call" | custom-call | flops 1073741824 | bytes 8388608 | tf_op jit(solution)/shard_map/pallas_call | solution.py:274
  27.3 1.4 %collective-permute-start.11 = (bf16[640,128]{1,0:T(8,128)(2,1)S(1)}, bf16[640,128]{1,0:T(8,128)(2,1)S(1)}, u32[]{:S(2)}, u32[]{:S(2)}) collective-permute-start(bf16[640,128]{1,0:T(8,128)(2,1)S(1)} %get-tuple-element.29), channel_id=1, source_target_pairs={{0,48},{16,0},{32,16},{48,32},{1,17},{17,33},{33,49},{49,1},{2,50}... | collective-permute-start | bytes 491528 | tf_op jit(solution)/shard_map/ppermute | solution.py:219
  28.7 1.3 %collective-permute-start.9 = (bf16[640,128]{1,0:T(8,128)(2,1)S(1)}, bf16[640,128]{1,0:T(8,128)(2,1)S(1)}, u32[]{:S(2)}, u32[]{:S(2)}) collective-permute-start(bf16[640,128]{1,0:T(8,128)(2,1)S(1)} %get-tuple-element.25.after), channel_id=1, source_target_pairs={{0,16},{16,32},{32,48},{48,0},{1,49},{17,1},{33,17},{49,33},{2,18}... | collective-permute-start | bytes 491528 | tf_op jit(solution)/shard_map/ppermute | solution.py:219
  30.0 0.6 %collective-permute-start.13 = (bf16[512,128]{1,0:T(8,128)(2,1)S(1)}, bf16[512,128]{1,0:T(8,128)(2,1)S(1)}, u32[]{:S(2)}, u32[]{:S(2)}) collective-permute-start(bf16[512,128]{1,0:T(8,128)(2,1)S(1)} %get-tuple-element.32), channel_id=1, source_target_pairs={{0,32},{16,48},{32,0},{48,16},{1,33},{17,49},{33,1},{49,17},{2,34}... | collective-permute-start | bytes 393224 | tf_op jit(solution)/shard_map/ppermute | solution.py:219
  30.6 2.0 %collective-permute-start.12 = (bf16[512,128]{1,0:T(8,128)(2,1)S(1)}, bf16[512,128]{1,0:T(8,128)(2,1)S(1)}, u32[]{:S(2)}, u32[]{:S(2)}) collective-permute-start(bf16[512,128]{1,0:T(8,128)(2,1)S(1)} %get-tuple-element.31), channel_id=1, source_target_pairs={{0,16},{16,32},{32,48},{48,0},{1,49},{17,1},{33,17},{49,33},{2,18}... | collective-permute-start | bytes 393224 | tf_op jit(solution)/shard_map/ppermute | solution.py:219
  32.6 0.6 %shard_map.91 = (f32[512,128]{1,0:T(8,128)S(1)}, f32[512,128]{1,0:T(8,128)S(1)}) custom-call(s32[1,1024]{1,0:T(1,128)S(4)} %get-tuple-element.20.order, bf16[32,128,128]{2,1,0:T(8,128)(2,1)S(1)} %get-tuple-element.23.grads, bf16[256,128,128]{2,1,0:T(8,128)(2,1)S(1)} %get-tuple-element.22.refs_9_.tiles, bf16[640,128]{1,0:T(8,128)(2,1)S(1)} %get-tuple-element.25.after), custom_call_target="tpu_custom_call" | custom-call | flops 1073741824 | bytes 8388608 | tf_op jit(solution)/shard_map/pallas_call | solution.py:281
  33.2 1.6 %collective-permute-done.9.r1 = bf16[640,128]{1,0:T(8,128)(2,1)S(1)} collective-permute-done((bf16[640,128]{1,0:T(8,128)(2,1)S(1)}, bf16[640,128]{1,0:T(8,128)(2,1)S(1)}, u32[]{:S(2)}, u32[]{:S(2)}) %collective-permute-start.9) | collective-permute-done | bytes 163872 | tf_op jit(solution)/shard_map/ppermute | solution.py:219
  34.9 7.2 %collective-permute-start.16 = (bf16[384,128]{1,0:T(8,128)(2,1)S(1)}, bf16[384,128]{1,0:T(8,128)(2,1)S(1)}, u32[]{:S(2)}, u32[]{:S(2)}) collective-permute-start(bf16[384,128]{1,0:T(8,128)(2,1)S(1)} %get-tuple-element.36), channel_id=1, source_target_pairs={{0,128},{64,192},{128,0},{192,64},{1,129},{65,193},{129,1},{193,65... | collective-permute-start | bytes 294920 | tf_op jit(solution)/shard_map/ppermute | solution.py:219
  42.1 2.0 %collective-permute-start.17 = (bf16[384,128]{1,0:T(8,128)(2,1)S(1)}, bf16[384,128]{1,0:T(8,128)(2,1)S(1)}, u32[]{:S(2)}, u32[]{:S(2)}) collective-permute-start(bf16[384,128]{1,0:T(8,128)(2,1)S(1)} %get-tuple-element.37), channel_id=1, source_target_pairs={{0,192},{64,0},{128,64},{192,128},{1,65},{65,129},{129,193},{193,1... | collective-permute-start | bytes 294920 | tf_op jit(solution)/shard_map/ppermute | solution.py:219
  44.2 2.7 %collective-permute-start.15 = (bf16[384,128]{1,0:T(8,128)(2,1)S(1)}, bf16[384,128]{1,0:T(8,128)(2,1)S(1)}, u32[]{:S(2)}, u32[]{:S(2)}) collective-permute-start(bf16[384,128]{1,0:T(8,128)(2,1)S(1)} %get-tuple-element.35), channel_id=1, source_target_pairs={{0,64},{64,128},{128,192},{192,0},{1,193},{65,1},{129,65},{193,129... | collective-permute-start | bytes 294920 | tf_op jit(solution)/shard_map/ppermute | solution.py:219
  46.9 1.4 %collective-permute-done.17.r3 = bf16[384,128]{1,0:T(8,128)(2,1)S(1)} collective-permute-done((bf16[384,128]{1,0:T(8,128)(2,1)S(1)}, bf16[384,128]{1,0:T(8,128)(2,1)S(1)}, u32[]{:S(2)}, u32[]{:S(2)}) %collective-permute-start.17) | collective-permute-done | bytes 98336 | tf_op jit(solution)/shard_map/ppermute | solution.py:219
  48.3 3.9 %collective-permute-done.15.r1 = bf16[384,128]{1,0:T(8,128)(2,1)S(1)} collective-permute-done((bf16[384,128]{1,0:T(8,128)(2,1)S(1)}, bf16[384,128]{1,0:T(8,128)(2,1)S(1)}, u32[]{:S(2)}, u32[]{:S(2)}) %collective-permute-start.15) | collective-permute-done | bytes 98336 | tf_op jit(solution)/shard_map/ppermute | solution.py:219
  52.1 0.7 %shard_map.94 = (bf16[256,128]{1,0:T(8,128)(2,1)}, f32[128,128]{1,0:T(8,128)}) custom-call(f32[256,128]{1,0:T(8,128)S(1)} %get-tuple-element.34.keep, bf16[128,128]{1,0:T(8,128)(2,1)S(1)} %get-tuple-element.30.weight_y, bf16[384,128]{1,0:T(8,128)(2,1)S(1)} %collective-permute-done.15.r1, bf16[384,128]{1,0:T(8,128)(2,1)S(1)} %collective-permute-done.16.r2, ...), custom_call_target="tpu_custom_call" | custom-call | tf_op jit(solution)/shard_map/pallas_call | solution.py:302
  (15 shorter events, 0.3 us)
Async XLA Ops:
  1.8 4.3 %collective-permute-start = (bf16[256,256]{1,0:T(8,128)(2,1)S(1)}, bf16[256,256]{1,0:T(8,128)(2,1)S(1)}, u32[]{:S(2)}, u32[]{:S(2)}) collective-permute-start(bf16[256,256]{1,0:T(8,128)(2,1)S(1)} %shard_map.87.own), channel_id=1, source_target_pairs={{0,1},{1,0},{2,3},{3,2},{4,5},{5,4},{6,7},{7,6},{8,9},{9,8},{10,11... | collective-permute-start | bytes 393224 | tf_op jit(solution)/shard_map/ppermute | solution.py:241
  6.7 10.0 %collective-permute-start.1 = (bf16[320,256]{1,0:T(8,128)(2,1)S(1)}, bf16[320,256]{1,0:T(8,128)(2,1)S(1)}, u32[]{:S(2)}, u32[]{:S(2)}) collective-permute-start(bf16[320,256]{1,0:T(8,128)(2,1)S(1)} %shard_map.88.refs_0_), channel_id=1, source_target_pairs={{1,9},{3,11},{5,13},{7,15},{9,1},{11,3},{13,5},{15,7},{17,25},{19,... | collective-permute-start | bytes 491528 | tf_op jit(solution)/shard_map/ppermute | solution.py:256
  8.6 8.0 %collective-permute-start.4 = (bf16[320,256]{1,0:T(8,128)(2,1)S(1)}, bf16[320,256]{1,0:T(8,128)(2,1)S(1)}, u32[]{:S(2)}, u32[]{:S(2)}) collective-permute-start(bf16[320,256]{1,0:T(8,128)(2,1)S(1)} %shard_map.88.refs_0_), channel_id=1, source_target_pairs={{0,6},{1,11},{2,0},{3,13},{4,2},{5,15},{6,4},{7,9},{8,14},{9,3},{1... | collective-permute-start | bytes 491528 | tf_op jit(solution)/shard_map/ppermute | solution.py:256
  9.5 8.3 %collective-permute-start.3 = (bf16[320,256]{1,0:T(8,128)(2,1)S(1)}, bf16[320,256]{1,0:T(8,128)(2,1)S(1)}, u32[]{:S(2)}, u32[]{:S(2)}) collective-permute-start(bf16[320,256]{1,0:T(8,128)(2,1)S(1)} %shard_map.88.refs_0_), channel_id=1, source_target_pairs={{0,4},{1,13},{2,6},{3,15},{4,0},{5,9},{6,2},{7,11},{8,12},{9,5},{1... | collective-permute-start | bytes 491528 | tf_op jit(solution)/shard_map/ppermute | solution.py:256
  13.1 6.1 %collective-permute-start.2 = (bf16[320,256]{1,0:T(8,128)(2,1)S(1)}, bf16[320,256]{1,0:T(8,128)(2,1)S(1)}, u32[]{:S(2)}, u32[]{:S(2)}) collective-permute-start(bf16[320,256]{1,0:T(8,128)(2,1)S(1)} %shard_map.88.refs_0_), channel_id=1, source_target_pairs={{0,2},{1,15},{2,4},{3,9},{4,6},{5,11},{6,0},{7,13},{8,10},{9,7},{1... | collective-permute-start | bytes 491528 | tf_op jit(solution)/shard_map/ppermute | solution.py:256
  16.7 4.3 %collective-permute-start.8 = (bf16[320,256]{1,0:T(8,128)(2,1)S(1)}, bf16[320,256]{1,0:T(8,128)(2,1)S(1)}, u32[]{:S(2)}, u32[]{:S(2)}) collective-permute-start(bf16[320,256]{1,0:T(8,128)(2,1)S(1)} %collective-permute-done.4.refs_4_), channel_id=1, source_target_pairs={{0,1},{1,0},{2,3},{3,2},{4,5},{5,4},{6,7},{7,6},{8,9},{9,8},{10,11... | collective-permute-start | bytes 491528 | tf_op jit(solution)/shard_map/ppermute | solution.py:262
  17.8 3.1 %collective-permute-start.7 = (bf16[320,256]{1,0:T(8,128)(2,1)S(1)}, bf16[320,256]{1,0:T(8,128)(2,1)S(1)}, u32[]{:S(2)}, u32[]{:S(2)}) collective-permute-start(bf16[320,256]{1,0:T(8,128)(2,1)S(1)} %collective-permute-done.3.refs_3_), channel_id=1, source_target_pairs={{0,1},{1,0},{2,3},{3,2},{4,5},{5,4},{6,7},{7,6},{8,9},{9,8},{10,11... | collective-permute-start | bytes 491528 | tf_op jit(solution)/shard_map/ppermute | solution.py:262
  19.3 2.7 %collective-permute-start.6 = (bf16[320,256]{1,0:T(8,128)(2,1)S(1)}, bf16[320,256]{1,0:T(8,128)(2,1)S(1)}, u32[]{:S(2)}, u32[]{:S(2)}) collective-permute-start(bf16[320,256]{1,0:T(8,128)(2,1)S(1)} %collective-permute-done.2.refs_2_), channel_id=1, source_target_pairs={{0,1},{1,0},{2,3},{3,2},{4,5},{5,4},{6,7},{7,6},{8,9},{9,8},{10,11... | collective-permute-start | bytes 491528 | tf_op jit(solution)/shard_map/ppermute | solution.py:262
  20.9 1.4 %collective-permute-start.5 = (bf16[320,256]{1,0:T(8,128)(2,1)S(1)}, bf16[320,256]{1,0:T(8,128)(2,1)S(1)}, u32[]{:S(2)}, u32[]{:S(2)}) collective-permute-start(bf16[320,256]{1,0:T(8,128)(2,1)S(1)} %collective-permute-done.1.refs_1_), channel_id=1, source_target_pairs={{0,1},{1,0},{2,3},{3,2},{4,5},{5,4},{6,7},{7,6},{8,9},{9,8},{10,11... | collective-permute-start | bytes 491528 | tf_op jit(solution)/shard_map/ppermute | solution.py:262
  23.6 9.5 %collective-permute-start.10 = (bf16[640,128]{1,0:T(8,128)(2,1)S(1)}, bf16[640,128]{1,0:T(8,128)(2,1)S(1)}, u32[]{:S(2)}, u32[]{:S(2)}) collective-permute-start(bf16[640,128]{1,0:T(8,128)(2,1)S(1)} %get-tuple-element.28), channel_id=1, source_target_pairs={{0,32},{16,48},{32,0},{48,16},{1,33},{17,49},{33,1},{49,17},{2,34}... | collective-permute-start | bytes 491528 | tf_op jit(solution)/shard_map/ppermute | solution.py:219
  27.3 6.0 %collective-permute-start.11 = (bf16[640,128]{1,0:T(8,128)(2,1)S(1)}, bf16[640,128]{1,0:T(8,128)(2,1)S(1)}, u32[]{:S(2)}, u32[]{:S(2)}) collective-permute-start(bf16[640,128]{1,0:T(8,128)(2,1)S(1)} %get-tuple-element.29), channel_id=1, source_target_pairs={{0,48},{16,0},{32,16},{48,32},{1,17},{17,33},{33,49},{49,1},{2,50}... | collective-permute-start | bytes 491528 | tf_op jit(solution)/shard_map/ppermute | solution.py:219
  28.7 6.1 %collective-permute-start.9 = (bf16[640,128]{1,0:T(8,128)(2,1)S(1)}, bf16[640,128]{1,0:T(8,128)(2,1)S(1)}, u32[]{:S(2)}, u32[]{:S(2)}) collective-permute-start(bf16[640,128]{1,0:T(8,128)(2,1)S(1)} %get-tuple-element.25.after), channel_id=1, source_target_pairs={{0,16},{16,32},{32,48},{48,0},{1,49},{17,1},{33,17},{49,33},{2,18}... | collective-permute-start | bytes 491528 | tf_op jit(solution)/shard_map/ppermute | solution.py:219
  30.0 14.1 %collective-permute-start.13 = (bf16[512,128]{1,0:T(8,128)(2,1)S(1)}, bf16[512,128]{1,0:T(8,128)(2,1)S(1)}, u32[]{:S(2)}, u32[]{:S(2)}) collective-permute-start(bf16[512,128]{1,0:T(8,128)(2,1)S(1)} %get-tuple-element.32), channel_id=1, source_target_pairs={{0,32},{16,48},{32,0},{48,16},{1,33},{17,49},{33,1},{49,17},{2,34}... | collective-permute-start | bytes 393224 | tf_op jit(solution)/shard_map/ppermute | solution.py:219
  30.6 13.5 %collective-permute-start.12 = (bf16[512,128]{1,0:T(8,128)(2,1)S(1)}, bf16[512,128]{1,0:T(8,128)(2,1)S(1)}, u32[]{:S(2)}, u32[]{:S(2)}) collective-permute-start(bf16[512,128]{1,0:T(8,128)(2,1)S(1)} %get-tuple-element.31), channel_id=1, source_target_pairs={{0,16},{16,32},{32,48},{48,0},{1,49},{17,1},{33,17},{49,33},{2,18}... | collective-permute-start | bytes 393224 | tf_op jit(solution)/shard_map/ppermute | solution.py:219
  33.1 11.0 %collective-permute-start.14 = (bf16[512,128]{1,0:T(8,128)(2,1)S(1)}, bf16[512,128]{1,0:T(8,128)(2,1)S(1)}, u32[]{:S(2)}, u32[]{:S(2)}) collective-permute-start(bf16[512,128]{1,0:T(8,128)(2,1)S(1)} %get-tuple-element.33), channel_id=1, source_target_pairs={{0,48},{16,0},{32,16},{48,32},{1,17},{17,33},{33,49},{49,1},{2,50}... | collective-permute-start | bytes 393224 | tf_op jit(solution)/shard_map/ppermute | solution.py:219
  34.9 12.0 %collective-permute-start.16 = (bf16[384,128]{1,0:T(8,128)(2,1)S(1)}, bf16[384,128]{1,0:T(8,128)(2,1)S(1)}, u32[]{:S(2)}, u32[]{:S(2)}) collective-permute-start(bf16[384,128]{1,0:T(8,128)(2,1)S(1)} %get-tuple-element.36), channel_id=1, source_target_pairs={{0,128},{64,192},{128,0},{192,64},{1,129},{65,193},{129,1},{193,65... | collective-permute-start | bytes 294920 | tf_op jit(solution)/shard_map/ppermute | solution.py:219
  42.1 6.2 %collective-permute-start.17 = (bf16[384,128]{1,0:T(8,128)(2,1)S(1)}, bf16[384,128]{1,0:T(8,128)(2,1)S(1)}, u32[]{:S(2)}, u32[]{:S(2)}) collective-permute-start(bf16[384,128]{1,0:T(8,128)(2,1)S(1)} %get-tuple-element.37), channel_id=1, source_target_pairs={{0,192},{64,0},{128,64},{192,128},{1,65},{65,129},{129,193},{193,1... | collective-permute-start | bytes 294920 | tf_op jit(solution)/shard_map/ppermute | solution.py:219
  44.2 8.0 %collective-permute-start.15 = (bf16[384,128]{1,0:T(8,128)(2,1)S(1)}, bf16[384,128]{1,0:T(8,128)(2,1)S(1)}, u32[]{:S(2)}, u32[]{:S(2)}) collective-permute-start(bf16[384,128]{1,0:T(8,128)(2,1)S(1)} %get-tuple-element.35), channel_id=1, source_target_pairs={{0,64},{64,128},{128,192},{192,0},{1,193},{65,1},{129,65},{193,129... | collective-permute-start | bytes 294920 | tf_op jit(solution)/shard_map/ppermute | solution.py:219
